TPU v7x, 512 devices: a whole 4x8x8 slice. The times are simulated.
512 devices in a mesh: row: 16 (over z, core), col: 8 (over y), depth: 4 (over x).
Axes of the slice: x: 4, y: 8, z: 8, core: 2. Of those that a mesh axis runs over, the one named last changes fastest.
Arguments:
- right_sides: float32 [64, 65536], P('depth', ('row', 'col')), may hold values from -12 to 12
- blocks: float32 [16, 8, 16, 256, 256], P('row', 'col'), may hold values from -0.06 to 6.1, as said below
- block_rows: int32 [16, 8, 16], P('row', 'col'), may hold values from 0 to 15, as said below
- block_cols: int32 [16, 8, 16], P('row', 'col'), may hold values from 0 to 31, as said below
- block_count: int32 [16, 8], P('row', 'col'), may hold values from 2 to 16
Outputs:
- solution: float32 [64, 65536], P('depth', ('row', 'col'))
- residual: float32 [64, 65536], P('depth', ('row', 'col'))
Inputs may be any that keep to these rules, and one draw needn't show every extreme that they name: Slot s < 2 of row index r and col index c holds the diagonal block with block_rows = c * 2 + s and block_cols = r * 2 + s. The valid later slots name distinct blocks whose I is below J. At slots from block_count on, block_rows and block_cols hold 0; blocks there hold arbitrary values and are not part of A. `block_cols`: see block_rows. Diagonal-slot blocks are symmetric; A is positive definite. Slots from block_count on are not part of A.
All inputs are finite; a program needn't handle non-finite values.
Results may differ from a plain program's by a relative error of at most 0.0003.
Values sent between devices are 32-bit elements; how exact they have to be, the bound alone decides.
A program may use at most 64 MiB of HBM per device.

v0:
```python
import functools

import jax
import jax.numpy as jnp
from jax import lax
from jax.sharding import Mesh
from jax.sharding import PartitionSpec as P

BLK = 256
ITERS = 2
SEG = 2
ROW = ("row_0", "row_1")
ROW_COL = ("row_0", "row_1", "col")


def copy_for_each(value, axis):
    copies = jnp.broadcast_to(value, (lax.axis_size(axis), *value.shape))
    return lax.all_to_all(copies, axis, split_axis=0, concat_axis=0, tiled=True)


def in_order(blocks, dim):
    lengths = list(blocks.shape[1:])
    lengths[dim] *= blocks.shape[0]
    return jnp.moveaxis(blocks, 0, dim).reshape(lengths)


def gathered_copies(value, axis, dim):
    blocks = copy_for_each(value, axis)
    return in_order(blocks, dim)


def in_blocks(value, dim, length):
    before, after = (value.shape[:dim], value.shape[dim + 1 :])
    return jnp.moveaxis(value.reshape(*before, length, -1, *after), dim, 0)


def summed_on_arrival(value, axis, dim):
    blocks = in_blocks(value, dim, lax.axis_size(axis))
    arrived = lax.all_to_all(blocks, axis, split_axis=0, concat_axis=0, tiled=True)
    return arrived.sum(axis=0)


def by_axis(value, axes):
    return functools.reduce(lax.psum, axes, value)


def per_device(right_sides, blocks, block_rows, block_cols, block_count):
    highest = lax.Precision.HIGHEST
    own_width = right_sides.shape[0]
    depth_index = lax.axis_index("depth")
    tile_blocks = blocks[0, 0]
    rows_here = block_rows[0, 0]
    cols_here = block_cols[0, 0]
    live_count = block_count[0, 0]
    row_span = SEG * lax.axis_size("col")
    col_span = SEG * lax.axis_size(ROW)
    slot_index = jnp.arange(tile_blocks.shape[0], dtype=jnp.int32)
    residual_all = gathered_copies(right_sides, "depth", 0)
    direction_all = residual_all
    solution = jnp.zeros_like(right_sides)
    current = by_axis(jnp.dot(residual_all, residual_all.T, precision=highest), ROW_COL)
    for iteration in range(ITERS):
        own_direction = lax.dynamic_slice_in_dim(
            direction_all, depth_index * own_width, own_width, 0
        )
        row_part = gathered_copies(own_direction, "col", 1).reshape(own_width, row_span, BLK)
        col_part = gathered_copies(own_direction, ROW, 1).reshape(own_width, col_span, BLK)
        live_mask = (slot_index < live_count).astype(jnp.float32)
        mirror_mask = live_mask * (slot_index >= SEG).astype(jnp.float32)
        toward_rows = jnp.einsum(
            "csk,smk->csm", col_part[:, cols_here], tile_blocks, precision=highest
        )
        toward_cols = jnp.einsum(
            "csm,smk->csk", row_part[:, rows_here], tile_blocks, precision=highest
        )
        toward_rows = toward_rows * live_mask[None, :, None]
        toward_cols = toward_cols * mirror_mask[None, :, None]
        row_select = (rows_here[:, None] == jnp.arange(row_span, dtype=jnp.int32)[None, :]).astype(
            jnp.float32
        )
        col_select = (cols_here[:, None] == jnp.arange(col_span, dtype=jnp.int32)[None, :]).astype(
            jnp.float32
        )
        row_terms = jnp.einsum("si,csm->cim", row_select, toward_rows, precision=highest)
        col_terms = jnp.einsum("sj,csk->cjk", col_select, toward_cols, precision=highest)
        row_sum = summed_on_arrival(row_terms.reshape(own_width, row_span * BLK), "col", 1)
        col_sum = summed_on_arrival(col_terms.reshape(own_width, col_span * BLK), ROW, 1)
        mapped = row_sum + col_sum
        mapped_all = gathered_copies(mapped, "depth", 0)
        curvature, cross_gram, image_gram = (
            by_axis(jnp.dot(direction_all, mapped_all.T, precision=highest), ROW_COL),
            by_axis(jnp.dot(residual_all, mapped_all.T, precision=highest), ROW_COL),
            by_axis(jnp.dot(mapped_all, mapped_all.T, precision=highest), ROW_COL),
        )
        step_size = jax.scipy.linalg.cho_solve((jnp.linalg.cholesky(curvature), True), current)
        own_step = lax.dynamic_slice_in_dim(step_size, depth_index * own_width, own_width, 1)
        solution = solution + lax.dot_general(
            own_step, direction_all, (((0,), (0,)), ((), ())), precision=highest
        )
        residual_all = residual_all - lax.dot_general(
            step_size, mapped_all, (((0,), (0,)), ((), ())), precision=highest
        )
        if iteration + 1 < ITERS:
            coupling = jnp.dot(cross_gram, step_size, precision=highest)
            quadratic = lax.dot_general(
                step_size,
                jnp.dot(image_gram, step_size, precision=highest),
                (((0,), (0,)), ((), ())),
                precision=highest,
            )
            renewed = current - coupling - coupling.T + quadratic
            conjugate = jax.scipy.linalg.cho_solve((jnp.linalg.cholesky(current), True), renewed)
            direction_all = residual_all + lax.dot_general(
                conjugate, direction_all, (((0,), (0,)), ((), ())), precision=highest
            )
            current = renewed
    own_residual = lax.dynamic_slice_in_dim(residual_all, depth_index * own_width, own_width, 0)
    return (solution, own_residual)


def solution(mesh):
    finer = Mesh(
        mesh.devices.reshape(8, 2, mesh.shape["col"], mesh.shape["depth"]),
        ("row_0", "row_1", "col", "depth"),
    )
    return jax.shard_map(
        per_device,
        mesh=finer,
        in_specs=(
            P("depth", ROW_COL),
            P(ROW, "col", None, None, None),
            P(ROW, "col", None),
            P(ROW, "col", None),
            P(ROW, "col"),
        ),
        out_specs=(P("depth", ROW_COL), P("depth", ROW_COL)),
        check_vma=False,
    )
```

profile of v0, /device:TPU:1, one launch (start us, length us, event | category | flops | bytes accessed | tf_op | source)
XLA Modules:
  0.0 342.1 jit_solution(4419644932302193203)
XLA Ops:
  12.4 6.8 %all-to-all-start.3 = ((f32[8,16,512]{2,1,0:T(8,128)}), f32[8,16,512]{2,1,0:T(8,128)S(1)}, u32[]{:S(2)}, u32[]{:S(2)}) async-start(f32[8,16,512]{2,1,0:T(8,128)} %broadcast_in_dim.17), calls=%async_computation.3 | async-start | bytes 524288 | tf_op jit(solution)/shard_map/all_to_all | solution.py:18
  19.9 8.7 %all-to-all-done.3 = f32[8,16,512]{2,1,0:T(8,128)S(1)} async-done(((f32[8,16,512]{2,1,0:T(8,128)}), f32[8,16,512]{2,1,0:T(8,128)S(1)}, u32[]{:S(2)}, u32[]{:S(2)}) %all-to-all-start.3) | async-done | bytes 262176 | tf_op jit(solution)/shard_map/all_to_all | solution.py:18
  29.5 13.8 %all-to-all-start.1 = ((f32[16,16,512]{2,1,0:T(8,128)}), f32[16,16,512]{2,1,0:T(8,128)S(1)}, u32[]{:S(2)}, u32[]{:S(2)}) async-start(f32[16,16,512]{2,1,0:T(8,128)} %broadcast_in_dim.16), calls=%async_computation.1 | async-start | bytes 1048576 | tf_op jit(solution)/shard_map/all_to_all | solution.py:18
  51.1 9.6 %all-to-all-done.1 = f32[16,16,512]{2,1,0:T(8,128)S(1)} async-done(((f32[16,16,512]{2,1,0:T(8,128)}), f32[16,16,512]{2,1,0:T(8,128)S(1)}, u32[]{:S(2)}, u32[]{:S(2)}) %all-to-all-start.1) | async-done | bytes 524320 | tf_op jit(solution)/shard_map/all_to_all | solution.py:18
  65.4 5.7 %fusion.11 = f32[16,16,256]{2,0,1:T(8,128)S(1)} fusion(f32[1,1,16,256,256]{4,3,2,1,0:T(8,128)} %param.9, f32[16,16,256]{2,1,0:T(8,128)S(1)} %gather_fusion, f32[16]{0:T(128)S(1)} %compare_convert_fusion), kind=kOutput, calls=%fused_computation.15 | convolution fusion | flops 201392128 | bytes 4718656 | tf_op jit(solution)/shard_map/csk,smk->csm/dot_general | solution.py:70
  72.5 8.3 %all-to-all-done.4 = f32[16,16,512]{2,1,0:T(8,128)S(1)} async-done(((f32[16,16,512]{2,1,0:T(8,128)}), f32[16,16,512]{2,1,0:T(8,128)S(1)}, u32[]{:S(2)}, u32[]{:S(2)}) %all-to-all-start.4) | async-done | bytes 524320 | tf_op jit(solution)/shard_map/all_to_all | solution.py:39
  84.3 11.6 %all-to-all-done.2 = f32[8,16,512]{2,1,0:T(8,128)S(1)} async-done(((f32[8,16,512]{2,1,0:T(8,128)}), f32[8,16,512]{2,1,0:T(8,128)S(1)}, u32[]{:S(2)}, u32[]{:S(2)}) %all-to-all-start.2) | async-done | bytes 262176 | tf_op jit(solution)/shard_map/all_to_all | solution.py:39
  105.2 21.0 %all-reduce.1 = (f32[64,64]{0,1:T(8,128)S(1)}, f32[64,64]{0,1:T(8,128)S(1)}, f32[64,64]{1,0:T(8,128)S(1)}) all-reduce(f32[64,64]{0,1:T(8,128)S(1)} %fusion.75, f32[64,64]{0,1:T(8,128)S(1)} %convolution_bitcast_fusion.4, f32[64,64]{1,0:T(8,128)S(1)} %fusion.77), channel_id=1, replica_groups=mesh['row_0'=8,'row_1'=2,'col'=8,'depth'=4] {'row_0'}, use_global_device_ids=true, to_apply=%region_7.9 | all-reduce | flops 12288 | bytes 98304 | tf_op jit(solution)/shard_map/psum | solution.py:44
  126.2 12.1 %all-reduce.2 = (f32[64,64]{0,1:T(8,128)S(1)}, f32[64,64]{0,1:T(8,128)S(1)}, f32[64,64]{1,0:T(8,128)S(1)}) all-reduce(f32[64,64]{0,1:T(8,128)S(1)} %get-tuple-element.7, f32[64,64]{0,1:T(8,128)S(1)} %get-tuple-element.8, f32[64,64]{1,0:T(8,128)S(1)} %get-tuple-element.9), channel_id=1, replica_groups=mesh['row_0'=8,'row_1'=2,'col'=8,'depth'=4] {'row_1'}, use_global_device_ids=true, to_apply=%region_8.10 | all-reduce | flops 12288 | bytes 98304 | tf_op jit(solution)/shard_map/psum | solution.py:44
  138.3 21.6 %all-reduce = (f32[64,64]{0,1:T(8,128)S(1)}, f32[64,64]{0,1:T(8,128)S(1)}, f32[64,64]{1,0:T(8,128)S(1)}) all-reduce(f32[64,64]{0,1:T(8,128)S(1)} %get-tuple-element.10, f32[64,64]{0,1:T(8,128)S(1)} %get-tuple-element.11, f32[64,64]{1,0:T(8,128)S(1)} %get-tuple-element.12), channel_id=1, replica_groups=mesh['row_0'=8,'row_1'=2,'col'=8,'depth'=4] {'col'}, use_global_device_ids=true, to_apply=%region_9.11 | all-reduce | flops 12288 | bytes 98304 | tf_op jit(solution)/shard_map/psum | solution.py:44
  160.0 5.8 %cholesky.59 = f32[64,64]{1,0:T(8,128)S(1)} custom-call(f32[64,64]{1,0:T(8,128)S(1)} %fusion.57), custom_call_target="Cholesky" | custom-call | tf_op jit(solution)/shard_map/jit(cholesky)/cholesky | solution.py:95
  167.2 4.9 %custom-call.9 = f32[1,64,64]{1,2,0:T(8,128)S(1)} custom-call(f32[1,64,64]{2,1,0:T(8,128)S(1)} %fusion.40), custom_call_target="InvertDiagBlocksLowerTriangular" | custom-call | tf_op jit(solution)/shard_map/jit(_cho_solve)/triangular_solve | solution.py:95
  173.5 5.8 %cholesky.70 = f32[64,64]{1,0:T(8,128)S(1)} custom-call(f32[64,64]{1,0:T(8,128)S(1)} %fusion.52), custom_call_target="Cholesky" | custom-call | tf_op jit(solution)/shard_map/jit(cholesky)/cholesky | solution.py:112
  186.6 12.5 %all_to_all.55 = f32[8,16,512]{2,1,0:T(8,128)S(1)} all-to-all(f32[8,16,512]{2,1,0:T(8,128)S(1)} %broadcast_in_dim.20), channel_id=1, replica_groups=mesh['row_0'=8,'row_1'=2,'col'=8,'depth'=4] {'col'}, dimensions={0} | all-to-all | bytes 524288 | tf_op jit(solution)/shard_map/all_to_all | solution.py:18
  200.0 14.3 %all-to-all-start.6 = ((f32[16,16,512]{2,1,0:T(8,128)}), f32[16,16,512]{2,1,0:T(8,128)S(1)}, u32[]{:S(2)}, u32[]{:S(2)}) async-start(f32[16,16,512]{2,1,0:T(8,128)} %broadcast_in_dim.19), calls=%async_computation.6 | async-start | bytes 1048576 | tf_op jit(solution)/shard_map/all_to_all | solution.py:18
  221.3 10.3 %all-to-all-done.6 = f32[16,16,512]{2,1,0:T(8,128)S(1)} async-done(((f32[16,16,512]{2,1,0:T(8,128)}), f32[16,16,512]{2,1,0:T(8,128)S(1)}, u32[]{:S(2)}, u32[]{:S(2)}) %all-to-all-start.6) | async-done | bytes 524320 | tf_op jit(solution)/shard_map/all_to_all | solution.py:18
  236.5 5.7 %fusion.23 = f32[16,16,256]{2,0,1:T(8,128)S(1)} fusion(f32[1,1,16,256,256]{4,3,2,1,0:T(8,128)} %param.9, f32[16,16,256]{2,1,0:T(8,128)S(1)} %gather_fusion.2, f32[16]{0:T(128)S(1)} %compare_convert_fusion), kind=kOutput, calls=%fused_computation.19 | convolution fusion | flops 201392128 | bytes 4718656 | tf_op jit(solution)/shard_map/csk,smk->csm/dot_general | solution.py:70
  243.6 8.2 %all-to-all-done.9 = f32[16,16,512]{2,1,0:T(8,128)S(1)} async-done(((f32[16,16,512]{2,1,0:T(8,128)}), f32[16,16,512]{2,1,0:T(8,128)S(1)}, u32[]{:S(2)}, u32[]{:S(2)}) %all-to-all-start.9) | async-done | bytes 524320 | tf_op jit(solution)/shard_map/all_to_all | solution.py:39
  255.2 11.4 %all-to-all-done.7 = f32[8,16,512]{2,1,0:T(8,128)S(1)} async-done(((f32[8,16,512]{2,1,0:T(8,128)}), f32[8,16,512]{2,1,0:T(8,128)S(1)}, u32[]{:S(2)}, u32[]{:S(2)}) %all-to-all-start.7) | async-done | bytes 262176 | tf_op jit(solution)/shard_map/all_to_all | solution.py:39
  275.7 20.1 %psum.102 = f32[64,64]{0,1:T(8,128)S(1)} all-reduce(f32[64,64]{0,1:T(8,128)S(1)} %fusion.79), channel_id=1, replica_groups=mesh['row_0'=8,'row_1'=2,'col'=8,'depth'=4] {'row_0'}, use_global_device_ids=true, to_apply=%region_15.0 | all-reduce | flops 4096 | bytes 32768 | tf_op jit(solution)/shard_map/psum | solution.py:44
  295.9 11.7 %psum.103 = f32[64,64]{0,1:T(8,128)S(1)} all-reduce(f32[64,64]{0,1:T(8,128)S(1)} %psum.102), channel_id=1, replica_groups=mesh['row_0'=8,'row_1'=2,'col'=8,'depth'=4] {'row_1'}, use_global_device_ids=true, to_apply=%region_16.0 | all-reduce | flops 4096 | bytes 32768 | tf_op jit(solution)/shard_map/psum | solution.py:44
  307.6 20.1 %psum.104 = f32[64,64]{0,1:T(8,128)S(1)} all-reduce(f32[64,64]{0,1:T(8,128)S(1)} %psum.103), channel_id=1, replica_groups=mesh['row_0'=8,'row_1'=2,'col'=8,'depth'=4] {'col'}, use_global_device_ids=true, to_apply=%region_17.0 | all-reduce | flops 4096 | bytes 32768 | tf_op jit(solution)/shard_map/psum | solution.py:44
  327.8 5.8 %cholesky.81 = f32[64,64]{1,0:T(8,128)S(1)} custom-call(f32[64,64]{1,0:T(8,128)S(1)} %fusion.47), custom_call_target="Cholesky" | custom-call | tf_op jit(solution)/shard_map/jit(cholesky)/cholesky | solution.py:95
  335.0 4.9 %custom-call.11 = f32[1,64,64]{1,2,0:T(8,128)S(1)} custom-call(f32[1,64,64]{2,1,0:T(8,128)S(1)} %fusion.42), custom_call_target="InvertDiagBlocksLowerTriangular" | custom-call | tf_op jit(solution)/shard_map/jit(_cho_solve)/triangular_solve | solution.py:95
  (100 shorter events, 79.5 us)
Async XLA Ops:
  2.0 9.7 %all-to-all-start = ((f32[4,16,512]{2,1,0:T(8,128)}), f32[4,16,512]{2,1,0:T(8,128)S(1)}, u32[]{:S(2)}, u32[]{:S(2)}) async-start(f32[4,16,512]{2,1,0:T(8,128)} %broadcast_in_dim.15), calls=%async_computation | async-start | bytes 262144 | tf_op jit(solution)/shard_map/all_to_all | solution.py:18
  12.4 16.2 %all-to-all-start.3 = ((f32[8,16,512]{2,1,0:T(8,128)}), f32[8,16,512]{2,1,0:T(8,128)S(1)}, u32[]{:S(2)}, u32[]{:S(2)}) async-start(f32[8,16,512]{2,1,0:T(8,128)} %broadcast_in_dim.17), calls=%async_computation.3 | async-start | bytes 524288 | tf_op jit(solution)/shard_map/all_to_all | solution.py:18
  19.9 29.4 %copy-start.1 = (s32[1,1,16]{2,1,0:T(1,128)S(1)}, s32[1,1,16]{2,1,0:T(1,128)}, u32[]{:S(2)}) copy-start(s32[1,1,16]{2,1,0:T(1,128)} %param.11) | copy-start | bytes 196
  29.5 31.1 %all-to-all-start.1 = ((f32[16,16,512]{2,1,0:T(8,128)}), f32[16,16,512]{2,1,0:T(8,128)S(1)}, u32[]{:S(2)}, u32[]{:S(2)}) async-start(f32[16,16,512]{2,1,0:T(8,128)} %broadcast_in_dim.16), calls=%async_computation.1 | async-start | bytes 1048576 | tf_op jit(solution)/shard_map/all_to_all | solution.py:18
  60.6 20.2 %all-to-all-start.4 = ((f32[16,16,512]{2,1,0:T(8,128)}), f32[16,16,512]{2,1,0:T(8,128)S(1)}, u32[]{:S(2)}, u32[]{:S(2)}) async-start(f32[16,16,512]{2,1,0:T(8,128)} %bitcast.155), calls=%async_computation.4 | async-start | bytes 1048576 | tf_op jit(solution)/shard_map/all_to_all | solution.py:39
  64.1 7.0 %copy-start = (s32[1,1,16]{2,1,0:T(1,128)S(1)}, s32[1,1,16]{2,1,0:T(1,128)}, u32[]{:S(2)}) copy-start(s32[1,1,16]{2,1,0:T(1,128)} %param.10) | copy-start | bytes 196
  80.8 15.0 %all-to-all-start.2 = ((f32[8,16,512]{2,1,0:T(8,128)}), f32[8,16,512]{2,1,0:T(8,128)S(1)}, u32[]{:S(2)}, u32[]{:S(2)}) async-start(f32[8,16,512]{2,1,0:T(8,128)} %bitcast.157), calls=%async_computation.2 | async-start | bytes 524288 | tf_op jit(solution)/shard_map/all_to_all | solution.py:39
  96.5 8.1 %all-to-all-start.5 = ((f32[4,16,512]{2,1,0:T(8,128)}), f32[4,16,512]{2,1,0:T(8,128)S(1)}, u32[]{:S(2)}, u32[]{:S(2)}) async-start(f32[4,16,512]{2,1,0:T(8,128)} %broadcast_in_dim.18), calls=%async_computation.5 | async-start | bytes 262144 | tf_op jit(solution)/shard_map/all_to_all | solution.py:18
  200.0 31.6 %all-to-all-start.6 = ((f32[16,16,512]{2,1,0:T(8,128)}), f32[16,16,512]{2,1,0:T(8,128)S(1)}, u32[]{:S(2)}, u32[]{:S(2)}) async-start(f32[16,16,512]{2,1,0:T(8,128)} %broadcast_in_dim.19), calls=%async_computation.6 | async-start | bytes 1048576 | tf_op jit(solution)/shard_map/all_to_all | solution.py:18
  231.5 20.2 %all-to-all-start.9 = ((f32[16,16,512]{2,1,0:T(8,128)}), f32[16,16,512]{2,1,0:T(8,128)S(1)}, u32[]{:S(2)}, u32[]{:S(2)}) async-start(f32[16,16,512]{2,1,0:T(8,128)} %bitcast.154), calls=%async_computation.9 | async-start | bytes 1048576 | tf_op jit(solution)/shard_map/all_to_all | solution.py:39
  251.8 14.9 %all-to-all-start.7 = ((f32[8,16,512]{2,1,0:T(8,128)}), f32[8,16,512]{2,1,0:T(8,128)S(1)}, u32[]{:S(2)}, u32[]{:S(2)}) async-start(f32[8,16,512]{2,1,0:T(8,128)} %bitcast.156), calls=%async_computation.7 | async-start | bytes 524288 | tf_op jit(solution)/shard_map/all_to_all | solution.py:39
  267.3 8.1 %all-to-all-start.10 = ((f32[4,16,512]{2,1,0:T(8,128)}), f32[4,16,512]{2,1,0:T(8,128)S(1)}, u32[]{:S(2)}, u32[]{:S(2)}) async-start(f32[4,16,512]{2,1,0:T(8,128)} %broadcast_in_dim.40), calls=%async_computation.10 | async-start | bytes 262144 | tf_op jit(solution)/shard_map/all_to_all | solution.py:18
where the time goes:
time: 348 us; the launch traced here: 342 us
  blocking collectives  119 us (34%)
  waiting for transfers between devices  82.1 us (24%)
  starting transfers between devices  60.3 us (17%)
  other arithmetic  37.7 us (11%)
  matrix products  26.8 us (8%)
  local copies, waits for them, and re-layouts  14.2 us (4%)
    psum x6, blocking collectives, by_axis(): return functools.reduce(lax.psum, axes, value)  107 us
    all_to_all x6, starting transfers between devices, copy_for_each(): return lax.all_to_all(copies, axis, split_axis=0, concat_axis=0, tiled=True)  46.4 us
    all_to_all x6, waiting for transfers between devices, copy_for_each(): return lax.all_to_all(copies, axis, split_axis=0, concat_axis=0, tiled=True)  42.5 us
    all_to_all x4, waiting for transfers between devices, summed_on_arrival(): lax.all_to_all(blocks, axis, split_axis=0, concat_axis=0, tiled=True)  39.5 us
    all_to_all x4, starting transfers between devices, summed_on_arrival(): lax.all_to_all(blocks, axis, split_axis=0, concat_axis=0, tiled=True)  14 us
    another operation x6, other arithmetic, per_device(): jnp.linalg.cholesky(curvature)  13 us
    all_to_all x1, blocking collectives, copy_for_each(): return lax.all_to_all(copies, axis, split_axis=0, concat_axis=0, tiled=True)  12.5 us
    dot_general x2, matrix products, per_device(): jnp.einsum('csk,smk->csm', col_part[:, cols_here], tile_blocks, precision...  11.4 us
  transfers between devices with their start and end apart: 10, of which 10 were waited for; matrix products, arithmetic and copies ran while one was open for 9% of the time, Pallas kernels for 0%

commit v1 on v0

v1 whole, which is shorter than its diff:
```python
import functools

import jax
import jax.numpy as jnp
from jax import lax
from jax.experimental import pallas as pl
from jax.experimental.pallas import tpu as pltpu
from jax.sharding import PartitionSpec as P

SEG = 2
MESH = pl.DeviceIdType.MESH
F32 = jnp.float32
BF16 = jnp.bfloat16


def hdot(a, b, dims):
    return lax.dot_general(
        a, b, ((dims[:1], dims[1:]), ((), ())),
        precision=lax.Precision.HIGHEST, preferred_element_type=F32,
    )


def split(v):
    hi = v.astype(BF16)
    return hi, (v - hi.astype(F32)).astype(BF16)


def eliminate(systems, n):
    m = systems[0].shape[1]
    down = lax.broadcasted_iota(jnp.int32, (n, m), 0)
    for k in range(n):
        after = []
        for a in systems:
            row = jnp.broadcast_to(a[k : k + 1, :], (n, m))
            col = jnp.broadcast_to(a[:, k : k + 1], (n, m))
            pivot = jnp.broadcast_to(a[k : k + 1, k : k + 1], (n, m))
            scaled = row / pivot
            after.append(jnp.where(down == k, scaled, a - col * scaled))
        systems = after
    return systems


def kernel(dims, rs_ref, blocks_hbm, rows_ref, cols_ref, count_ref, x_ref, r_ref,
           bbuf, bhi, blo, rowg0, rowg1, colg0, colg1, allg, tr, tc, rt, ct, yb, zb, sb, ga, gb, gz, gy, gx, n1, n2, d2, ad2,
           sem_b, s_row, s_col, s_fwd, s_all, r_row, r_col, r_sib, r_all,
           s_y, s_s, s_z, r_y, r_s, r_z, s_g, r_g, s_n, r_n):
    NZ, NC, ND, W, BLK, SLOTS = dims
    NF = W * ND
    rowg, colg = (rowg0, rowg1), (colg0, colg1)
    ri, ci, di = lax.axis_index("row"), lax.axis_index("col"), lax.axis_index("depth")
    zi, ki = ri // 2, ri % 2
    sib = (zi * 2 + 1 - ki, ci, di)

    def zpeer(i):
        return lax.rem(zi + i, NZ)

    def ypeer(i):
        return lax.rem(ci + i, NC)

    def xpeer(i):
        return lax.rem(di + i, ND)

    def remote(src, dst, send, recv, where):
        copy = pltpu.make_async_remote_copy(
            src_ref=src, dst_ref=dst, send_sem=send, recv_sem=recv, device_id=where, device_id_type=MESH
        )
        copy.start()

    def taken(ref, sem):
        pltpu.make_async_copy(ref, ref, sem).wait()

    load_blocks = pltpu.make_async_copy(blocks_hbm, bbuf, sem_b)
    load_blocks.start()

    barrier = pltpu.get_barrier_semaphore()
    pl.semaphore_signal(barrier, inc=1, device_id=sib, device_id_type=MESH)
    for i in range(1, NC):
        pl.semaphore_signal(barrier, inc=1, device_id=(ri, ypeer(i), di), device_id_type=MESH)
    for i in range(1, NZ):
        for k in range(2):
            pl.semaphore_signal(barrier, inc=1, device_id=(zpeer(i) * 2 + k, ci, di), device_id_type=MESH)
    for j in range(1, ND):
        pl.semaphore_signal(barrier, inc=1, device_id=(zi * 2 + 1 - ki, ci, xpeer(j)), device_id_type=MESH)
        for i in range(NC):
            pl.semaphore_signal(barrier, inc=1, device_id=(ri, ypeer(i), xpeer(j)), device_id_type=MESH)
    greeted = 1 + (NC - 1) + 2 * (NZ - 1) + (ND - 1) * (NC + 1)

    mine = pl.ds(pl.multiple_of(di * W, W), W)

    def publish(it, parts):
        for s in range(SEG):
            rowg[it][ci, s] = parts[s]
            colg[it][ki, zi, s] = parts[s]
            allg[it, s, mine, :] = parts[s]

    def gather_start(it):
        def z_send(i, _):
            remote(colg[it].at[ki, zi], colg[it].at[ki, zi], s_col.at[it], r_col.at[it, zi],
                   (zpeer(i) * 2 + ki, ci, di))
            return 0

        def y_send(i, _):
            remote(rowg[it].at[ci], rowg[it].at[ci], s_row.at[it], r_row.at[it], (ri, ypeer(i), di))
            return 0

        lax.fori_loop(1, NZ, z_send, 0)
        lax.fori_loop(1, NC, y_send, 0)
        remote(colg[it].at[ki, zi], colg[it].at[ki, zi], s_fwd.at[it], r_sib.at[it], sib)
        part = allg.at[it, :, mine, :]

        def x_send(i, _):
            remote(part, part, s_all.at[it], r_all.at[it], (ri, ci, xpeer(i)))
            return 0

        lax.fori_loop(1, ND, x_send, 0)

    def forward(it):
        def one(i, _):
            j = lax.rem(zi + NZ - i, NZ)
            here = colg[it].at[ki, j]
            taken(here, r_col.at[it, j])
            remote(here, here, s_fwd.at[it], r_sib.at[it], sib)
            return 0

        lax.fori_loop(1, NZ, one, 0)

    def live(ref, s):
        return jnp.where(s < count_ref[0, 0], ref[0, 0, s], -1)

    def place(j):
        return (j // 2) % 2, j // 4, j % 2

    def apply3(v, s, turned):
        hi, lo = split(v)
        both = jnp.concatenate([hi, lo], 0)
        d = (((1,), (1 if turned else 0,)), ((), ()))
        a = lax.dot_general(both, bhi[s], d, preferred_element_type=F32)
        b = lax.dot_general(hi, blo[s], d, preferred_element_type=F32)
        return a[:W] + a[W:] + b

    def matvec(it):
        taken(rowg[it].at[pl.ds(0, NC - 1)], r_row.at[it])
        for s in range(SEG, SLOTS):
            i = rows_ref[0, 0, s]
            tc[s] = apply3(rowg[it][i // SEG, i % SEG], s, False)
        names = [live(cols_ref, s) for s in range(SLOTS)]

        def col_target(k):
            def body(t, _):
                z, seg = t // SEG, t % SEG
                j = z * 4 + k * 2 + seg
                acc = jnp.zeros((W, BLK), F32)
                for s in range(SEG, SLOTS):
                    acc = acc + jnp.where(names[s] == j, 1.0, 0.0) * tc[s]
                ct[it, k, z, seg] = acc
                return 0

            lax.fori_loop(0, NZ * SEG, body, 0)

        col_target(1 - ki)
        remote(ct.at[it, 1 - ki], sb.at[it], s_s.at[it], r_s.at[it], sib)
        col_target(ki)
        taken(colg[it].at[1 - ki], r_sib.at[it])
        for s in range(SLOTS):
            k, z, seg = place(cols_ref[0, 0, s])
            tr[s] = apply3(colg[it][k, z, seg], s, True)
        taken(sb.at[it], r_s.at[it])
        for z in range(NZ):
            ct[it, ki, z] = ct[it, ki, z] + sb[it, z]

        def z_send(i, _):
            to = zpeer(i)
            remote(ct.at[it, ki, to], zb.at[it, zi], s_z.at[it], r_z.at[it], (to * 2 + ki, ci, di))
            return 0

        lax.fori_loop(1, NZ, z_send, 0)
        labels = [live(rows_ref, s) for s in range(SLOTS)]

        def row_target(t, _):
            c = ypeer(t // SEG + 1)
            seg = t % SEG
            acc = jnp.zeros((W, BLK), F32)
            for s in range(SLOTS):
                acc = acc + jnp.where(labels[s] == c * SEG + seg, 1.0, 0.0) * tr[s]
            rt[it, c, seg] = acc
            return 0

        lax.fori_loop(0, NC * SEG, row_target, 0)

        def y_send(i, _):
            to = ypeer(i)
            remote(rt.at[it, to], yb.at[it, ci], s_y.at[it], r_y.at[it], (ri, to, di))
            return 0

        lax.fori_loop(1, NC, y_send, 0)

    def collect(it):
        parts = [rt[it, ci, s] + ct[it, ki, zi, s] for s in range(SEG)]
        taken(yb.at[it, pl.ds(0, NC - 1)], r_y.at[it])
        taken(zb.at[it, pl.ds(0, NZ - 1)], r_z.at[it])
        for i in range(1, NC):
            parts = [parts[s] + yb[it, ypeer(i), s] for s in range(SEG)]
        for i in range(1, NZ):
            parts = [parts[s] + zb[it, zpeer(i), s] for s in range(SEG)]
        return parts

    publish(0, [rs_ref[:, s * BLK : (s + 1) * BLK] for s in range(SEG)])
    pl.semaphore_wait(barrier, greeted)
    gather_start(0)
    load_blocks.wait()

    def cut(s, _):
        hi, lo = split(bbuf[s])
        bhi[s] = hi
        blo[s] = lo
        return 0

    lax.fori_loop(0, SLOTS, cut, 0)
    forward(0)
    matvec(0)
    publish(1, collect(0))
    gather_start(1)

    taken(allg.at[0, :, pl.ds(0, W * (ND - 1)), :], r_all.at[0])
    taken(allg.at[1, :, pl.ds(0, W * (ND - 1)), :], r_all.at[1])
    gram = jnp.zeros((2 * W, 2 * NF), F32)
    for s in range(SEG):
        left = jnp.concatenate([allg[0, s, mine, :], allg[1, s, mine, :]], 0)
        right = jnp.concatenate([allg[0, s], allg[1, s]], 0)
        gram = gram + hdot(left, right, (1, 1))
    ga[0] = gram[:W]
    ga[1] = gram[W:]
    remote(ga.at[1 - ki], gb, s_g.at[0], r_g.at[0], sib)
    forward(1)
    taken(gb, r_g.at[0])
    gz[zi] = ga[ki] + gb[...]

    def gz_send(i, _):
        remote(gz.at[zi], gz.at[zi], s_g.at[1], r_g.at[1], (zpeer(i) * 2 + ki, ci, di))
        return 0

    lax.fori_loop(1, NZ, gz_send, 0)
    matvec(1)
    taken(gz.at[pl.ds(0, NZ - 1)], r_g.at[1])
    gy[ci] = sum(gz[z] for z in range(NZ))

    def gy_send(i, _):
        remote(gy.at[ci], gy.at[ci], s_g.at[2], r_g.at[2], (ri, ypeer(i), di))
        return 0

    lax.fori_loop(1, NC, gy_send, 0)
    taken(gy.at[pl.ds(0, NC - 1)], r_g.at[2])
    gx[ki * ND + di] = sum(gy[c] for c in range(NC))
    piece = gx.at[ki * ND + di]
    remote(piece, piece, s_g.at[3], r_g.at[3], sib)
    for i in range(1, ND):
        for k in range(2):
            remote(piece, piece, s_g.at[3], r_g.at[3], (zi * 2 + lax.rem(ki + k, 2), ci, xpeer(i)))
    taken(gx.at[pl.ds(0, 2 * ND - 1)], r_g.at[3])

    low = gx[pl.ds(0, ND)].reshape(NF, 2 * NF)
    high = gx[pl.ds(ND, ND)].reshape(NF, 2 * NF)
    m0, m1, m2 = low[:, :NF], low[:, NF:], high[:, NF:]
    eye = (
        lax.broadcasted_iota(jnp.int32, (NF, NF), 0) == lax.broadcasted_iota(jnp.int32, (NF, NF), 1)
    ).astype(F32)
    own = (
        lax.broadcasted_iota(jnp.int32, (W, NF), 0) + di * W == lax.broadcasted_iota(jnp.int32, (W, NF), 1)
    ).astype(F32)
    first, second = eliminate(
        [jnp.concatenate([m1, m0], 1), jnp.concatenate([m0, eye], 1)], NF
    )
    step, inverse = first[:, NF:], second[:, NF:]
    coupling = hdot(m1, step, (1, 0))
    renewed = m0 - coupling - coupling.T + hdot(step, hdot(m2, step, (1, 0)), (0, 0))
    lift = eye + hdot(inverse, renewed, (1, 0))
    known = hdot(hdot(lift, m1, (0, 0)) - hdot(step, m2, (0, 0)), lift, (1, 0))
    renewed_own = hdot(renewed, own, (1, 1))
    step_own = hdot(own, step, (1, 1))
    for s in range(SEG):
        d2[s] = hdot(lift, allg[0, s], (0, 0)) - hdot(step, allg[1, s], (0, 0))
        x_ref[:, s * BLK : (s + 1) * BLK] = hdot(step_own, allg[0, s], (1, 0))
        r_ref[:, s * BLK : (s + 1) * BLK] = allg[0, s, mine, :] - hdot(step_own, allg[1, s], (1, 0))

    last = collect(1)
    for s in range(SEG):
        allg[2, s, mine, :] = last[s]
    part = allg.at[2, :, mine, :]
    cross = hdot(last[0], d2[0], (1, 1)) + hdot(last[1], d2[1], (1, 1))
    n1[ri] = jnp.concatenate([cross[: W // 2], cross[W // 2 :]], 1)

    remote(n1.at[ri], n1.at[ri], s_n.at[0], r_n.at[0], sib)
    for i in range(1, NZ):
        for k in range(2):
            remote(n1.at[ri], n1.at[ri], s_n.at[0], r_n.at[0], (zpeer(i) * 2 + k, ci, di))

    def x_send(i, _):
        remote(part, part, s_all.at[2], r_all.at[2], (ri, ci, xpeer(i)))
        return 0

    lax.fori_loop(1, ND, x_send, 0)
    taken(n1.at[pl.ds(0, 2 * NZ - 1)], r_n.at[0])
    n2[ci * ND + di] = sum(n1[r] for r in range(2 * NZ))
    for j in range(ND):
        for i in range(NC):
            if i or j:
                remote(n2.at[ci * ND + di], n2.at[ci * ND + di], s_n.at[1], r_n.at[1], (ri, ypeer(i), xpeer(j)))
    taken(allg.at[2, :, pl.ds(0, W * (ND - 1)), :], r_all.at[2])
    for s in range(SEG):
        ad2[s] = hdot(lift, allg[1, s], (0, 0)) - hdot(step, allg[2, s], (0, 0))
    taken(n2.at[pl.ds(0, NC * ND - 1)], r_n.at[1])
    total = sum(n2[pl.ds(c * ND, ND)] for c in range(NC))
    rows = []
    for d in range(ND):
        rows += [total[d, :, :NF], total[d, :, NF:]]
    cross = jnp.concatenate(rows, 0)
    curvature = known - hdot(cross, step, (0, 0))
    pad = jnp.zeros((NF, NF - W), F32)
    (done,) = eliminate([jnp.concatenate([curvature, renewed_own, pad], 1)], NF)
    step_own = done[:, NF : NF + W]
    for s in range(SEG):
        span = slice(s * BLK, (s + 1) * BLK)
        x_ref[:, span] = x_ref[:, span] + hdot(step_own, d2[s], (0, 0))
        r_ref[:, span] = r_ref[:, span] - hdot(step_own, ad2[s], (0, 0))

    for it in range(2):
        taken(rowg[it].at[pl.ds(0, NC - 1)], s_row.at[it])
        taken(colg[it].at[0, pl.ds(0, NZ - 1)], s_col.at[it])
        taken(colg[it].at[0], s_fwd.at[it])
        taken(yb.at[it, pl.ds(0, NC - 1)], s_y.at[it])
        taken(sb.at[it], s_s.at[it])
        taken(zb.at[it, pl.ds(0, NZ - 1)], s_z.at[it])
    for it in range(3):
        taken(allg.at[it, :, pl.ds(0, W * (ND - 1)), :], s_all.at[it])
    taken(gb, s_g.at[0])
    taken(gz.at[pl.ds(0, NZ - 1)], s_g.at[1])
    taken(gy.at[pl.ds(0, NC - 1)], s_g.at[2])
    taken(gx.at[pl.ds(0, 2 * ND - 1)], s_g.at[3])
    taken(n1.at[pl.ds(0, 2 * NZ - 1)], s_n.at[0])
    taken(n2.at[pl.ds(0, NC * ND - 1)], s_n.at[1])


def per_device(dims, right_sides, blocks, block_rows, block_cols, block_count):
    NZ, NC, ND, W, BLK, SLOTS = dims
    NF = W * ND
    vm = lambda *shape: pltpu.VMEM(shape, F32)
    dma = lambda *shape: pltpu.SemaphoreType.DMA(shape)
    spec = lambda space: pl.BlockSpec(memory_space=space)
    shape = jax.ShapeDtypeStruct(right_sides.shape, F32)
    return pl.pallas_call(
        functools.partial(kernel, dims),
        out_shape=(shape, shape),
        in_specs=[spec(pltpu.VMEM), spec(pl.ANY), spec(pltpu.SMEM), spec(pltpu.SMEM), spec(pltpu.SMEM)],
        out_specs=(spec(pltpu.VMEM), spec(pltpu.VMEM)),
        scratch_shapes=[
            vm(SLOTS, BLK, BLK), pltpu.VMEM((SLOTS, BLK, BLK), BF16), pltpu.VMEM((SLOTS, BLK, BLK), BF16),
            *[vm(NC, SEG, W, BLK)] * 2, *[vm(2, NZ, SEG, W, BLK)] * 2, vm(3, SEG, NF, BLK),
            vm(SLOTS, W, BLK), vm(SLOTS, W, BLK),
            vm(2, NC, SEG, W, BLK), vm(2, 2, NZ, SEG, W, BLK),
            vm(2, NC, SEG, W, BLK), vm(2, NZ, SEG, W, BLK), vm(2, NZ, SEG, W, BLK),
            vm(2, W, 2 * NF), vm(W, 2 * NF), vm(NZ, W, 2 * NF), vm(NC, W, 2 * NF), vm(2 * ND, W, 2 * NF),
            vm(2 * NZ, W // 2, 2 * NF), vm(NC * ND, W // 2, 2 * NF),
            vm(SEG, NF, BLK), vm(SEG, NF, BLK),
            pltpu.SemaphoreType.DMA,
            dma(2), dma(2), dma(2), dma(3), dma(2), dma(2, NZ), dma(2), dma(3),
            dma(2), dma(2), dma(2), dma(2), dma(2), dma(2), dma(4), dma(4), dma(2), dma(2),
        ],
        compiler_params=pltpu.CompilerParams(
            collective_id=0, has_side_effects=True, vmem_limit_bytes=48 * 2**20
        ),
        name="block_cg",
    )(right_sides, blocks.reshape(SLOTS, BLK, BLK), block_rows, block_cols, block_count)


def solution(mesh):
    rows, cols, depth = (mesh.shape[a] for a in ("row", "col", "depth"))

    def whole(right_sides, blocks, block_rows, block_cols, block_count):
        dims = (rows // 2, cols, depth, right_sides.shape[0] // depth, blocks.shape[3], blocks.shape[2])
        return jax.shard_map(
            functools.partial(per_device, dims),
            mesh=mesh,
            in_specs=(
                P("depth", ("row", "col")),
                P("row", "col", None, None, None),
                P("row", "col", None),
                P("row", "col", None),
                P("row", "col"),
            ),
            out_specs=(P("depth", ("row", "col")), P("depth", ("row", "col"))),
            check_vma=False,
        )(right_sides, blocks, block_rows, block_cols, block_count)

    return whole
```

time: 348 us -> 105 us (0.30); the launches traced: 342 us -> 105 us
  blocking collectives: 119 us -> 0 us
  Pallas kernels: 0 us -> 98 us
  waiting for transfers between devices: 82.1 us -> 0 us
  starting transfers between devices: 60.3 us -> 0 us
  other arithmetic: 37.7 us -> 0 us
  matrix products: 26.8 us -> 0 us
  local copies, waits for them, and re-layouts: 14.2 us -> 5.48 us
    psum x6 -> x0, blocking collectives: 107 us -> none  [by_axis(): return functools.reduce(lax.psum, axes, value)]
    pallas_call x0 -> x1, Pallas kernels: none -> 98 us  [per_device(): pl.pallas_call(functools.partial(kernel, dims), out_shape=(shape, shape),...]
    all_to_all x10 -> x0, waiting for transfers between devices: 82.1 us -> none  [the longest x6 42.5 us: copy_for_each(): return lax.all_to_all(copies, axis, split_axis=0, concat_axis=0, tiled=True)]
    all_to_all x10 -> x0, starting transfers between devices: 60.3 us -> none  [the longest x6 46.4 us: copy_for_each(): return lax.all_to_all(copies, axis, split_axis=0, concat_axis=0, tiled=True)]
    another operation x15 -> x0, other arithmetic: 36.2 us -> none  [the longest x6 13 us: per_device(): jnp.linalg.cholesky(curvature)]
    dot_general x20 -> x0, matrix products: 25.4 us -> none  [the longest x2 11.4 us: per_device(): jnp.einsum('csk,smk->csm', col_part[:, cols_here], tile_blocks, precision...]
    all_to_all x1 -> x0, blocking collectives: 12.5 us -> none  [copy_for_each(): return lax.all_to_all(copies, axis, split_axis=0, concat_axis=0, tiled=True)]
    another operation x16 -> x0, local copies, waits for them, and re-layouts: 5.53 us -> none  [the longest x8 4.36 us: in_blocks(): return jnp.moveaxis(value.reshape(*before, length, -1, *after), dim, 0)]
  transfers between devices with their start and end apart: 10 -> 0, of which waited for: 10 -> 0; matrix products, arithmetic and copies ran while one was open for 9% -> 0% of each run, Pallas kernels for 0% -> 0%
where the time goes in v1:
time: 105 us
  Pallas kernels  98 us (93%)
  local copies, waits for them, and re-layouts  5.48 us (5%)
  between operations  1.3 us (1%)
    pallas_call x1, Pallas kernels, per_device(): pl.pallas_call(functools.partial(kernel, dims), out_shape=(shape, shape),...  98 us
    unnamed x10, local copies, waits for them, and re-layouts  5.48 us

profile of v1, /device:TPU:1, one launch (start us, length us, event | category | flops | bytes accessed | tf_op | source)
XLA Modules:
  0.0 104.8 jit_solution(12545818279678127056)
XLA Ops:
  1.3 0.0 copy-start
  1.3 2.2 %copy-done = f32[1,1,16,256,256]{4,3,2,1,0:T(8,128)S(1)} copy-done((f32[1,1,16,256,256]{4,3,2,1,0:T(8,128)S(1)}, f32[1,1,16,256,256]{4,3,2,1,0:T(8,128)}, u32[]{:S(2)}) %copy-start) | copy-done | bytes 4194328
  3.5 0.0 copy-start.1
  3.5 0.8 copy-done.1
  4.2 0.0 copy-start.2
  4.2 0.7 copy-done.2
  4.9 0.0 copy-start.3
  4.9 0.7 copy-done.3
  5.5 98.0 %block_cg.1 = (f32[16,512]{1,0:T(8,128)S(1)}, f32[16,512]{1,0:T(8,128)S(1)}) custom-call(f32[16,512]{1,0:T(8,128)S(1)} %copy-done.1, f32[16,256,256]{2,1,0:T(8,128)S(1)} %bitcast.1, s32[1,1,16]{2,1,0:T(1,128)S(1)} %copy-done.2, s32[1,1,16]{2,1,0:T(1,128)S(1)} %copy-done.3, s32[1,1]{1,0:T(1,128)S(6)} %copy.9.count_ref), custom_call_target="tpu_custom_call" | custom-call | tf_op jit(solution)/shard_map/block_cg/pallas_call | solution.py:350
  103.6 0.6 copy.10
  104.2 0.6 copy.11
Async XLA Ops:
  1.3 2.2 %copy-start = (f32[1,1,16,256,256]{4,3,2,1,0:T(8,128)S(1)}, f32[1,1,16,256,256]{4,3,2,1,0:T(8,128)}, u32[]{:S(2)}) copy-start(f32[1,1,16,256,256]{4,3,2,1,0:T(8,128)} %param.6) | copy-start | bytes 12582916
  3.5 0.8 copy-start.1
  4.2 0.7 copy-start.2
  4.9 0.7 copy-start.3

commit v2 on v0

v2 whole, which is shorter than its diff:
```python
import functools

import jax
import jax.numpy as jnp
from jax import lax
from jax.experimental import pallas as pl
from jax.experimental.pallas import tpu as pltpu
from jax.sharding import PartitionSpec as P

SEG = 2
MESH = pl.DeviceIdType.MESH
F32 = jnp.float32
BF16 = jnp.bfloat16
PIVOTS = 8


def hdot(a, b, dims):
    return lax.dot_general(
        a, b, ((dims[:1], dims[1:]), ((), ())),
        precision=lax.Precision.HIGHEST, preferred_element_type=F32,
    )


def bdot(a, b):
    return jnp.dot(a, b, preferred_element_type=F32)


def split(v):
    hi = v.astype(BF16)
    return hi, (v - hi.astype(F32)).astype(BF16)


def far_first(n):
    return sorted(range(1, n), key=lambda i: (-min(i, n - i), i))


def eliminate(systems, n):
    m = systems[0].shape[1]
    down = lax.broadcasted_iota(jnp.int32, (n, m), 0)
    spread = range(PIVOTS)
    for k in range(0, n, PIVOTS):
        after = []
        for a in systems:
            rows = [jnp.broadcast_to(a[k + i : k + i + 1, :], (8, m)) for i in spread]
            p = [[jnp.broadcast_to(rows[i][:, k + j : k + j + 1], (8, m)) for j in spread] for i in spread]
            cols = [jnp.broadcast_to(a[:, k + j : k + j + 1], (n, m)) for j in spread]
            for q in spread:
                inverse = 1.0 / p[q][q]
                rows[q] = rows[q] * inverse
                for j in range(q + 1, PIVOTS):
                    p[q][j] = p[q][j] * inverse
                for i in spread:
                    if i != q:
                        for j in range(q + 1, PIVOTS):
                            p[i][j] = p[i][j] - p[i][q] * p[q][j]
                        rows[i] = rows[i] - p[i][q] * rows[q]
            full = [jnp.concatenate([r] * (n // 8), 0) for r in rows]
            new = a
            for j in spread:
                new = new - cols[j] * full[j]
            for j in spread:
                new = jnp.where(down == k + j, full[j], new)
            after.append(new)
        systems = after
    return systems


def kernel(dims, rs_hbm, blocks_hbm, rows_s, cols_s, count_s, x_ref, r_ref,
           rs, bbuf, bhi, blo, thi, tlo, er, ec,
           rowg0, rowg1, colg0, colg1, allg, tr, tc, rt, ct, yb, zb, sb,
           ga, gb, gz, gy, gx, ny, nz, nx, d2, ad2,
           sem_l, s_row, s_col, s_fwd, s_all, r_row, r_col, r_sib, r_all,
           s_y, s_s, s_z, r_y, r_s, r_z, s_g, r_g, s_n, r_n):
    NZ, NC, ND, W, BLK, SLOTS = dims
    NF = W * ND
    CH = SEG * W
    rowg, colg = (rowg0, rowg1), (colg0, colg1)
    ri, ci, di = lax.axis_index("row"), lax.axis_index("col"), lax.axis_index("depth")
    zi, ki = ri // 2, ri % 2
    sib = (zi * 2 + 1 - ki, ci, di)

    def zpeer(i):
        return lax.rem(zi + i, NZ)

    def ypeer(i):
        return lax.rem(ci + i, NC)

    def xpeer(i):
        return lax.rem(di + i, ND)

    def on_z(i):
        return (zpeer(i) * 2 + ki, ci, di)

    def on_y(i):
        return (ri, ypeer(i), di)

    def on_x(i):
        return (ri, ci, xpeer(i))

    def remote(src, dst, send, recv, where):
        pltpu.make_async_remote_copy(
            src_ref=src, dst_ref=dst, send_sem=send, recv_sem=recv, device_id=where, device_id_type=MESH
        ).start()

    def taken(ref, sem):
        pltpu.make_async_copy(ref, ref, sem).wait()

    loads = [
        pltpu.make_async_copy(src, dst, sem_l.at[i])
        for i, (src, dst) in enumerate([
            (rs_hbm, rs), (blocks_hbm, bbuf),
        ])
    ]
    for load in loads:
        load.start()

    with jax.named_scope("greet"):
        barrier = pltpu.get_barrier_semaphore()
        greeted = [on_z(i) for i in far_first(NZ)] + [on_y(i) for i in far_first(NC)]
        greeted += [on_x(i) for i in far_first(ND)]
        greeted += [(zi * 2 + 1 - ki, ci, xpeer(i)) for i in far_first(ND)] + [sib]
        for where in greeted:
            pl.semaphore_signal(barrier, inc=1, device_id=where, device_id_type=MESH)

    mine = pl.ds(pl.multiple_of(di * W, W), W)

    def publish(it, part):
        rowg[it][ci] = part.reshape(SEG, W, BLK)
        colg[it][ki, zi] = part.reshape(SEG, W, BLK)
        for s in range(SEG):
            allg[it, s, mine, :] = part[s * W : (s + 1) * W]

    def z_gather(it, i):
        remote(colg[it].at[ki, zi], colg[it].at[ki, zi], s_col.at[it], r_col.at[it, zi], on_z(i))

    def y_gather(it, i):
        remote(rowg[it].at[ci], rowg[it].at[ci], s_row.at[it], r_row.at[it], on_y(i))

    def x_gather(it):
        part = allg.at[it, :, mine, :]
        for i in far_first(ND):
            remote(part, part, s_all.at[it], r_all.at[it], on_x(i))

    def to_sibling(it, z):
        here = colg[it].at[ki, z]
        remote(here, here, s_fwd.at[it], r_sib.at[it], sib)

    def forward(it, order):
        for i in order:
            j = lax.rem(zi + NZ - i, NZ)
            taken(colg[it].at[ki, j], r_col.at[it, j])
            to_sibling(it, j)

    def apply3(v, high, low):
        hi, lo = split(v)
        a = bdot(jnp.concatenate([hi, lo], 0), high)
        return a[:W] + a[W:] + bdot(hi, low)

    def chosen(select, terms):
        hi, lo = split(terms)
        return bdot(select, hi) + bdot(select, lo)

    def rows_part(it):
        for s in range(SLOTS):
            j = cols_s[0, 0, s]
            tr[s * W : (s + 1) * W] = apply3(colg[it][(j // SEG) % 2, j // (2 * SEG), j % SEG], thi[s], tlo[s])
        rt[it] = chosen(er[...], tr[...]).reshape(NC, CH, BLK)
        for i in far_first(NC):
            remote(rt.at[it, ypeer(i)], yb.at[it, ci], s_y.at[it], r_y.at[it], on_y(i))

    def cols_first(it):
        for s in range(SEG, SLOTS):
            i = rows_s[0, 0, s]
            tc[s * W : (s + 1) * W] = apply3(rowg[it][i // SEG, i % SEG], bhi[s], blo[s])
        ct[it, 1 - ki] = chosen(ec[1 - ki], tc[...]).reshape(NZ, CH, BLK)
        remote(ct.at[it, 1 - ki], sb.at[it], s_s.at[it], r_s.at[it], sib)

    def cols_second(it):
        own = chosen(ec[ki], tc[...]).reshape(NZ, CH, BLK)
        taken(sb.at[it], r_s.at[it])
        ct[it, ki] = own + sb[it]
        for i in far_first(NZ):
            remote(ct.at[it, ki, zpeer(i)], zb.at[it, zi], s_z.at[it], r_z.at[it], on_z(i))

    def row_sum(it):
        taken(yb.at[it, pl.ds(0, NC - 1)], r_y.at[it])
        part = rt[it, ci]
        for i in range(1, NC):
            part = part + yb[it, ypeer(i)]
        return part

    def col_sum(it):
        taken(zb.at[it, pl.ds(0, NZ - 1)], r_z.at[it])
        part = ct[it, ki, zi]
        for i in range(1, NZ):
            part = part + zb[it, zpeer(i)]
        return part

    loads[0].wait()
    publish(0, jnp.concatenate([rs[:, s * BLK : (s + 1) * BLK] for s in range(SEG)], 0))
    with jax.named_scope("greeted"):
        pl.semaphore_wait(barrier, len(greeted))
    with jax.named_scope("send0"):
        for i in far_first(max(NZ, NC)):
            if i < NZ:
                z_gather(0, i)
            if i < NC:
                y_gather(0, i)
        to_sibling(0, zi)
        x_gather(0)

    with jax.named_scope("prepare"):
        for load in loads[1:]:
            load.wait()

        def chooser(ref, first, names):
            shape = (names.shape[0], SLOTS * W)
            across = lax.broadcasted_iota(jnp.int32, shape, 1)
            field = lax.broadcasted_iota(jnp.int32, shape, 0) % W
            wanted = jnp.full(shape, -1, jnp.int32)
            for s in range(first, SLOTS):
                name = jnp.where(s < count_s[0, 0], ref[0, 0, s], -1)
                wanted = jnp.where(across // W == s, name, wanted)
            return jnp.where((wanted == names) & (across % W == field), 1.0, 0.0).astype(BF16)

        block = lax.broadcasted_iota(jnp.int32, (NC * CH, SLOTS * W), 0) // W
        er[...] = chooser(rows_s, 0, block)
        block = lax.broadcasted_iota(jnp.int32, (NZ * CH, SLOTS * W), 0) // W
        for k in range(2):
            ec[k] = chooser(cols_s, SEG, (block // SEG) * 4 + k * 2 + block % SEG)
        tc[:CH] = jnp.zeros((CH, BLK), F32)

        def cut(s, _):
            stored = bbuf[s]
            hi, lo = split(stored)
            bhi[s] = hi
            blo[s] = lo
            hi, lo = split(stored.T)
            thi[s] = hi
            tlo[s] = lo
            return 0

        lax.fori_loop(0, SLOTS, cut, 0)
    with jax.named_scope("forward0"):
        forward(0, range(1, NZ))
    with jax.named_scope("wait_y0"):
        taken(rowg[0].at[pl.ds(0, NC - 1)], r_row.at[0])
    with jax.named_scope("cols0"):
        cols_first(0)
    with jax.named_scope("wait_sib0"):
        taken(colg[0].at[1 - ki], r_sib.at[0])
    with jax.named_scope("rows0"):
        rows_part(0)
    with jax.named_scope("cols_second0"):
        cols_second(0)
    with jax.named_scope("collect0"):
        publish(1, row_sum(0) + col_sum(0))
    with jax.named_scope("send1"):
        for i in far_first(NZ):
            z_gather(1, i)
        x_gather(1)
        to_sibling(1, zi)
        for i in far_first(NC):
            y_gather(1, i)

    with jax.named_scope("gram"):
        taken(allg.at[0, :, pl.ds(0, W * (ND - 1)), :], r_all.at[0])
        taken(allg.at[1, :, pl.ds(0, W * (ND - 1)), :], r_all.at[1])
        gram = jnp.zeros((2 * W, 2 * NF), F32)
        for s in range(SEG):
            left = jnp.concatenate([allg[0, s, mine, :], allg[1, s, mine, :]], 0)
            right = jnp.concatenate([allg[0, s], allg[1, s]], 0)
            gram = gram + hdot(left, right, (1, 1))
        ga[0] = gram[:W]
        ga[1] = gram[W:]
        remote(ga.at[1 - ki], gb, s_g.at[0], r_g.at[0], sib)
    order = sorted(range(1, NZ), key=lambda i: min(i, NZ - i))
    with jax.named_scope("forward1"):
        forward(1, order[: len(order) // 2])
        taken(gb, r_g.at[0])
        gz[zi] = ga[ki] + gb[...]
        for i in far_first(NZ):
            remote(gz.at[zi], gz.at[zi], s_g.at[1], r_g.at[1], on_z(i))
        forward(1, order[len(order) // 2 :])
    with jax.named_scope("wait_sib1"):
        taken(colg[1].at[1 - ki], r_sib.at[1])
    with jax.named_scope("rows1"):
        rows_part(1)
    with jax.named_scope("wait_y1"):
        taken(rowg[1].at[pl.ds(0, NC - 1)], r_row.at[1])
    with jax.named_scope("cols1"):
        cols_first(1)
    with jax.named_scope("gram_z"):
        taken(gz.at[pl.ds(0, NZ - 1)], r_g.at[1])
        gy[ci] = sum(gz[z] for z in range(NZ))
        for i in far_first(NC):
            remote(gy.at[ci], gy.at[ci], s_g.at[2], r_g.at[2], on_y(i))
    with jax.named_scope("cols_second1"):
        cols_second(1)

    with jax.named_scope("row_sum1"):
        part = row_sum(1)
    with jax.named_scope("cross"):
        half = part - 0.5 * tr[:CH]
        cross = sum(hdot(half[s * W : (s + 1) * W], allg[1, s], (1, 1)) for s in range(SEG))
        ny[ci] = jnp.concatenate([cross[: W // 2], cross[W // 2 :]], 1)
        for i in far_first(NC):
            remote(ny.at[ci], ny.at[ci], s_n.at[0], r_n.at[0], on_y(i))
    with jax.named_scope("gram_y"):
        taken(gy.at[pl.ds(0, NC - 1)], r_g.at[2])
        piece = gx.at[ki * ND + di]
        gx[ki * ND + di] = sum(gy[c] for c in range(NC))
        beside = [on_x(i) for i in far_first(ND)] + [(zi * 2 + 1 - ki, ci, xpeer(i)) for i in far_first(ND)] + [sib]
        for where in beside:
            remote(piece, piece, s_g.at[3], r_g.at[3], where)
    with jax.named_scope("col_sum1"):
        part = part + col_sum(1)
        for s in range(SEG):
            allg[2, s, mine, :] = part[s * W : (s + 1) * W]
        x_gather(2)
    with jax.named_scope("cross_y"):
        taken(ny.at[pl.ds(0, NC - 1)], r_n.at[0])
        nz[zi] = sum(ny[c] for c in range(NC))
        for i in far_first(NZ):
            remote(nz.at[zi], nz.at[zi], s_n.at[1], r_n.at[1], on_z(i))
    with jax.named_scope("gram_x"):
        taken(gx.at[pl.ds(0, 2 * ND - 1)], r_g.at[3])
    with jax.named_scope("solve1"):
        low = gx[pl.ds(0, ND)].reshape(NF, 2 * NF)
        high = gx[pl.ds(ND, ND)].reshape(NF, 2 * NF)
        m0, m1, m2 = low[:, :NF], low[:, NF:], high[:, NF:]
        eye = (
            lax.broadcasted_iota(jnp.int32, (NF, NF), 0) == lax.broadcasted_iota(jnp.int32, (NF, NF), 1)
        ).astype(F32)
        own = (
            lax.broadcasted_iota(jnp.int32, (W, NF), 0) + di * W == lax.broadcasted_iota(jnp.int32, (W, NF), 1)
        ).astype(F32)
        first, second = eliminate(
            [jnp.concatenate([m1, m0], 1), jnp.concatenate([m0, eye], 1)], NF
        )
        step, inverse = first[:, NF:], second[:, NF:]
    with jax.named_scope("algebra"):
        coupling = hdot(m1, step, (1, 0))
        pushed = hdot(m2, step, (1, 0))
        renewed = m0 - coupling - coupling.T + hdot(step, pushed, (0, 0))
        lift = eye + hdot(inverse, renewed, (1, 0))
        mixed = hdot(lift, pushed, (0, 0))
        known = hdot(lift, hdot(m1, lift, (1, 0)), (0, 0)) - mixed - mixed.T
        renewed_own = hdot(renewed, own, (1, 1))
        step_own = hdot(own, step, (1, 1))
    with jax.named_scope("cross_z"):
        taken(nz.at[pl.ds(0, NZ - 1)], r_n.at[1])
        piece = nx.at[ki * ND + di]
        nx[ki * ND + di] = sum(nz[z] for z in range(NZ))
        for where in beside:
            remote(piece, piece, s_n.at[2], r_n.at[2], where)
    with jax.named_scope("direction2"):
        for s in range(SEG):
            d2[s] = hdot(lift, allg[0, s], (0, 0)) - hdot(step, allg[1, s], (0, 0))
            x_ref[:, s * BLK : (s + 1) * BLK] = hdot(step_own, allg[0, s], (1, 0))
            r_ref[:, s * BLK : (s + 1) * BLK] = allg[0, s, mine, :] - hdot(step_own, allg[1, s], (1, 0))
    with jax.named_scope("image2"):
        taken(allg.at[2, :, pl.ds(0, W * (ND - 1)), :], r_all.at[2])
        for s in range(SEG):
            ad2[s] = hdot(lift, allg[1, s], (0, 0)) - hdot(step, allg[2, s], (0, 0))
    with jax.named_scope("cross_x"):
        taken(nx.at[pl.ds(0, 2 * ND - 1)], r_n.at[2])
    with jax.named_scope("solve2"):
        rows = []
        for d in range(ND):
            total = nx[d] + nx[ND + d]
            rows += [total[:, :NF], total[:, NF:]]
        cross = jnp.concatenate(rows, 0)
        curvature = known + hdot(step, hdot(cross + cross.T, step, (1, 0)), (0, 0))
        pad = jnp.zeros((NF, NF - W), F32)
        (done,) = eliminate([jnp.concatenate([curvature, renewed_own, pad], 1)], NF)
        step_own = done[:, NF : NF + W]
    with jax.named_scope("finish"):
        for s in range(SEG):
            span = slice(s * BLK, (s + 1) * BLK)
            x_ref[:, span] = x_ref[:, span] + hdot(step_own, d2[s], (0, 0))
            r_ref[:, span] = r_ref[:, span] - hdot(step_own, ad2[s], (0, 0))

    with jax.named_scope("sent"):
        for it in range(2):
            taken(rowg[it].at[pl.ds(0, NC - 1)], s_row.at[it])
            taken(colg[it].at[0, pl.ds(0, NZ - 1)], s_col.at[it])
            taken(colg[it].at[0], s_fwd.at[it])
            taken(yb.at[it, pl.ds(0, NC - 1)], s_y.at[it])
            taken(sb.at[it], s_s.at[it])
            taken(zb.at[it, pl.ds(0, NZ - 1)], s_z.at[it])
        for it in range(3):
            taken(allg.at[it, :, pl.ds(0, W * (ND - 1)), :], s_all.at[it])
        taken(gb, s_g.at[0])
        taken(gz.at[pl.ds(0, NZ - 1)], s_g.at[1])
        taken(gy.at[pl.ds(0, NC - 1)], s_g.at[2])
        taken(gx.at[pl.ds(0, 2 * ND - 1)], s_g.at[3])
        taken(ny.at[pl.ds(0, NC - 1)], s_n.at[0])
        taken(nz.at[pl.ds(0, NZ - 1)], s_n.at[1])
        taken(nx.at[pl.ds(0, 2 * ND - 1)], s_n.at[2])


def per_device(dims, right_sides, blocks, block_rows, block_cols, block_count):
    NZ, NC, ND, W, BLK, SLOTS = dims
    NF = W * ND
    CH = SEG * W
    vm = lambda *shape: pltpu.VMEM(shape, F32)
    half = lambda *shape: pltpu.VMEM(shape, BF16)
    dma = lambda *shape: pltpu.SemaphoreType.DMA(shape)
    shape = jax.ShapeDtypeStruct(right_sides.shape, F32)
    return pl.pallas_call(
        functools.partial(kernel, dims),
        out_shape=(shape, shape),
        in_specs=[pl.BlockSpec(memory_space=pl.ANY)] * 2 + [pl.BlockSpec(memory_space=pltpu.SMEM)] * 3,
        out_specs=(pl.BlockSpec(memory_space=pltpu.VMEM),) * 2,
        scratch_shapes=[
            vm(*right_sides.shape),
            vm(SLOTS, BLK, BLK), *[half(SLOTS, BLK, BLK)] * 4, half(NC * CH, SLOTS * W), half(2, NZ * CH, SLOTS * W),
            *[vm(NC, SEG, W, BLK)] * 2, *[vm(2, NZ, SEG, W, BLK)] * 2, vm(3, SEG, NF, BLK),
            vm(SLOTS * W, BLK), vm(SLOTS * W, BLK),
            vm(2, NC, CH, BLK), vm(2, 2, NZ, CH, BLK), vm(2, NC, CH, BLK), vm(2, NZ, CH, BLK), vm(2, NZ, CH, BLK),
            vm(2, W, 2 * NF), vm(W, 2 * NF), vm(NZ, W, 2 * NF), vm(NC, W, 2 * NF), vm(2 * ND, W, 2 * NF),
            vm(NC, W // 2, 2 * NF), vm(NZ, W // 2, 2 * NF), vm(2 * ND, W // 2, 2 * NF),
            vm(SEG, NF, BLK), vm(SEG, NF, BLK),
            dma(2),
            dma(2), dma(2), dma(2), dma(3), dma(2), dma(2, NZ), dma(2), dma(3),
            dma(2), dma(2), dma(2), dma(2), dma(2), dma(2), dma(4), dma(4), dma(3), dma(3),
        ],
        compiler_params=pltpu.CompilerParams(
            collective_id=0, has_side_effects=True, vmem_limit_bytes=62 * 2**20
        ),
        name="block_cg",
    )(right_sides, blocks.reshape(SLOTS, BLK, BLK), block_rows, block_cols, block_count)


def solution(mesh):
    rows, cols, depth = (mesh.shape[a] for a in ("row", "col", "depth"))

    def whole(right_sides, blocks, block_rows, block_cols, block_count):
        dims = (rows // 2, cols, depth, right_sides.shape[0] // depth, blocks.shape[3], blocks.shape[2])
        return jax.shard_map(
            functools.partial(per_device, dims),
            mesh=mesh,
            in_specs=(
                P("depth", ("row", "col")),
                P("row", "col", None, None, None),
                P("row", "col", None),
                P("row", "col", None),
                P("row", "col"),
            ),
            out_specs=(P("depth", ("row", "col")), P("depth", ("row", "col"))),
            check_vma=False,
        )(right_sides, blocks, block_rows, block_cols, block_count)

    return whole
```

time: 348 us -> 75.7 us (0.22); the launches traced: 342 us -> 75.5 us
  blocking collectives: 119 us -> 0 us
  waiting for transfers between devices: 82.1 us -> 0 us
  Pallas kernels: 0 us -> 71.4 us
  starting transfers between devices: 60.3 us -> 0 us
  other arithmetic: 37.7 us -> 0 us
  matrix products: 26.8 us -> 0 us
  local copies, waits for them, and re-layouts: 14.2 us -> 2.75 us
    psum x6 -> x0, blocking collectives: 107 us -> none  [by_axis(): return functools.reduce(lax.psum, axes, value)]
    all_to_all x10 -> x0, waiting for transfers between devices: 82.1 us -> none  [the longest x6 42.5 us: copy_for_each(): return lax.all_to_all(copies, axis, split_axis=0, concat_axis=0, tiled=True)]
    pallas_call x0 -> x1, Pallas kernels: none -> 71.4 us  [per_device(): pl.pallas_call(functools.partial(kernel, dims), out_shape=(shape, shape),...]
    all_to_all x10 -> x0, starting transfers between devices: 60.3 us -> none  [the longest x6 46.4 us: copy_for_each(): return lax.all_to_all(copies, axis, split_axis=0, concat_axis=0, tiled=True)]
    another operation x15 -> x0, other arithmetic: 36.2 us -> none  [the longest x6 13 us: per_device(): jnp.linalg.cholesky(curvature)]
    dot_general x20 -> x0, matrix products: 25.4 us -> none  [the longest x2 11.4 us: per_device(): jnp.einsum('csk,smk->csm', col_part[:, cols_here], tile_blocks, precision...]
    all_to_all x1 -> x0, blocking collectives: 12.5 us -> none  [copy_for_each(): return lax.all_to_all(copies, axis, split_axis=0, concat_axis=0, tiled=True)]
    another operation x16 -> x0, local copies, waits for them, and re-layouts: 5.53 us -> none  [the longest x8 4.36 us: in_blocks(): return jnp.moveaxis(value.reshape(*before, length, -1, *after), dim, 0)]
  transfers between devices with their start and end apart: 10 -> 0, of which waited for: 10 -> 0; matrix products, arithmetic and copies ran while one was open for 9% -> 0% of each run, Pallas kernels for 0% -> 0%
where the time goes in v2:
time: 75.7 us; the launch traced here: 75.5 us
  Pallas kernels  71.4 us (94%)
  local copies, waits for them, and re-layouts  2.75 us (4%)
  between operations  1.29 us (2%)
    pallas_call x1, Pallas kernels, per_device(): pl.pallas_call(functools.partial(kernel, dims), out_shape=(shape, shape),...  71.4 us
    unnamed x2, local copies, waits for them, and re-layouts  2.75 us

profile of v2, /device:TPU:1, one launch (start us, length us, event | category | flops | bytes accessed | tf_op | source)
XLA Modules:
  0.0 75.5 jit_solution(1681195482735595964)
XLA Ops:
  1.3 71.4 %block_cg.1 = (f32[16,512]{1,0:T(8,128)}, f32[16,512]{1,0:T(8,128)}) custom-call(f32[16,512]{1,0:T(8,128)} %rs_hbm.1, f32[16,256,256]{2,1,0:T(8,128)} %bitcast.1, s32[1,1,16]{2,1,0:T(1,128)} %rows_s.1, s32[1,1,16]{2,1,0:T(1,128)} %cols_s.1, s32[1,1]{1,0:T(1,128)S(6)} %copy.9.count_s), custom_call_target="tpu_custom_call" | custom-call | tf_op jit(solution)/shard_map/block_cg/pallas_call | solution.py:411
  72.7 1.4 %copy.10 = f32[16,512]{1,0:T(8,128)} copy(f32[16,512]{1,0:T(8,128)} %get-tuple-element.4) | data formatting | bytes 65536
  74.1 1.4 %copy.11 = f32[16,512]{1,0:T(8,128)} copy(f32[16,512]{1,0:T(8,128)} %get-tuple-element.5) | data formatting | bytes 65536

commit v3 on v2

--- a/solution.py
+++ b/solution.py
@@ -67,9 +67,9 @@
 
 def kernel(dims, rs_hbm, blocks_hbm, rows_s, cols_s, count_s, x_ref, r_ref,
            rs, bbuf, bhi, blo, thi, tlo, er, ec,
-           rowg0, rowg1, colg0, colg1, allg, tr, tc, rt, ct, yb, zb, sb,
+           rowg0, rowg1, colg0, colg1, allg, rowall, tr, tc, rt, ct, yb, zb, sb,
            ga, gb, gz, gy, gx, ny, nz, nx, d2, ad2,
-           sem_l, s_row, s_col, s_fwd, s_all, r_row, r_col, r_sib, r_all,
+           sem_l, s_row, s_col, s_fwd, s_all, s_wide, r_row, r_col, r_sib, r_all, r_wide,
            s_y, s_s, s_z, r_y, r_s, r_z, s_g, r_g, s_n, r_n):
     NZ, NC, ND, W, BLK, SLOTS = dims
     NF = W * ND
@@ -134,7 +134,7 @@
         remote(colg[it].at[ki, zi], colg[it].at[ki, zi], s_col.at[it], r_col.at[it, zi], on_z(i))
 
     def y_gather(it, i):
-        remote(rowg[it].at[ci], rowg[it].at[ci], s_row.at[it], r_row.at[it], on_y(i))
+        remote(rowg[it].at[ci], rowg[it].at[ci], s_row.at[it], r_row.at[it, ci], on_y(i))
 
     def x_gather(it):
         part = allg.at[it, :, mine, :]
@@ -145,11 +145,22 @@
         here = colg[it].at[ki, z]
         remote(here, here, s_fwd.at[it], r_sib.at[it], sib)
 
-    def forward(it, order):
-        for i in order:
+    def forward(it, i):
+        if i < NZ:
             j = lax.rem(zi + NZ - i, NZ)
             taken(colg[it].at[ki, j], r_col.at[it, j])
             to_sibling(it, j)
+
+    def arrive(it, i):
+        c = lax.rem(ci + NC - i, NC)
+        taken(rowg[it].at[c], r_row.at[it, c])
+        return c
+
+    def widen(i):
+        if i < NC:
+            c = arrive(1, i)
+            for j in far_first(ND):
+                remote(rowg[1].at[c], rowall.at[c, :, mine, :], s_wide, r_wide, on_x(j))
 
     def apply3(v, high, low):
         hi, lo = split(v)
@@ -165,6 +176,8 @@
             j = cols_s[0, 0, s]
             tr[s * W : (s + 1) * W] = apply3(colg[it][(j // SEG) % 2, j // (2 * SEG), j % SEG], thi[s], tlo[s])
         rt[it] = chosen(er[...], tr[...]).reshape(NC, CH, BLK)
+
+    def rows_leave(it):
         for i in far_first(NC):
             remote(rt.at[it, ypeer(i)], yb.at[it, ci], s_y.at[it], r_y.at[it], on_y(i))
 
@@ -195,6 +208,8 @@
         for i in range(1, NZ):
             part = part + zb[it, zpeer(i)]
         return part
+
+    nearest = sorted(range(1, max(NZ, NC)), key=lambda i: min(i, max(NZ, NC) - i))
 
     loads[0].wait()
     publish(0, jnp.concatenate([rs[:, s * BLK : (s + 1) * BLK] for s in range(SEG)], 0))
@@ -242,27 +257,35 @@
 
         lax.fori_loop(0, SLOTS, cut, 0)
     with jax.named_scope("forward0"):
-        forward(0, range(1, NZ))
+        for i in nearest:
+            forward(0, i)
     with jax.named_scope("wait_y0"):
-        taken(rowg[0].at[pl.ds(0, NC - 1)], r_row.at[0])
+        for i in range(1, NC):
+            arrive(0, i)
     with jax.named_scope("cols0"):
         cols_first(0)
     with jax.named_scope("wait_sib0"):
         taken(colg[0].at[1 - ki], r_sib.at[0])
     with jax.named_scope("rows0"):
         rows_part(0)
+        rows_leave(0)
     with jax.named_scope("cols_second0"):
         cols_second(0)
     with jax.named_scope("collect0"):
         publish(1, row_sum(0) + col_sum(0))
     with jax.named_scope("send1"):
-        for i in far_first(NZ):
-            z_gather(1, i)
         x_gather(1)
+        for i in far_first(max(NZ, NC)):
+            if i < NC:
+                y_gather(1, i)
+            if i < NZ:
+                z_gather(1, i)
         to_sibling(1, zi)
-        for i in far_first(NC):
-            y_gather(1, i)
-
+
+    with jax.named_scope("forward1"):
+        for i in nearest[: len(nearest) // 2]:
+            widen(i)
+            forward(1, i)
     with jax.named_scope("gram"):
         taken(allg.at[0, :, pl.ds(0, W * (ND - 1)), :], r_all.at[0])
         taken(allg.at[1, :, pl.ds(0, W * (ND - 1)), :], r_all.at[1])
@@ -274,38 +297,59 @@
         ga[0] = gram[:W]
         ga[1] = gram[W:]
         remote(ga.at[1 - ki], gb, s_g.at[0], r_g.at[0], sib)
-    order = sorted(range(1, NZ), key=lambda i: min(i, NZ - i))
-    with jax.named_scope("forward1"):
-        forward(1, order[: len(order) // 2])
+    with jax.named_scope("forward1_more"):
+        for i in nearest[len(nearest) // 2 : -1]:
+            widen(i)
+            forward(1, i)
         taken(gb, r_g.at[0])
         gz[zi] = ga[ki] + gb[...]
         for i in far_first(NZ):
             remote(gz.at[zi], gz.at[zi], s_g.at[1], r_g.at[1], on_z(i))
-        forward(1, order[len(order) // 2 :])
+        widen(nearest[-1])
+        forward(1, nearest[-1])
+        for i in range(1, NC):
+            c = ypeer(i)
+            rowall[c, :, mine, :] = rowg[1][c]
+        rowall[ci] = allg[1]
     with jax.named_scope("wait_sib1"):
         taken(colg[1].at[1 - ki], r_sib.at[1])
     with jax.named_scope("rows1"):
         rows_part(1)
-    with jax.named_scope("wait_y1"):
-        taken(rowg[1].at[pl.ds(0, NC - 1)], r_row.at[1])
-    with jax.named_scope("cols1"):
-        cols_first(1)
+
+    with jax.named_scope("cross"):
+        taken(rowall.at[pl.ds(0, NC - 1), :, pl.ds(0, W * (ND - 1)), :], r_wide)
+        cross = jnp.zeros((2 * W, NF), F32)
+        rest = jnp.zeros((W, NF), F32)
+        for i in range(NC):
+            c = ypeer(i)
+            term = rt[1, c] if i else rt[1, c] - 0.5 * tr[:CH]
+            for s in range(SEG):
+                hi, lo = split(term[s * W : (s + 1) * W])
+                high, low = split(rowall[c, s])
+                turned = (((1,), (1,)), ((), ()))
+                cross = cross + lax.dot_general(
+                    jnp.concatenate([hi, lo], 0), high, turned, preferred_element_type=F32
+                )
+                rest = rest + lax.dot_general(hi, low, turned, preferred_element_type=F32)
+        cross = cross[:W] + cross[W:] + rest
+        ny[ci] = jnp.concatenate([cross[: W // 2], cross[W // 2 :]], 1)
+        for i in far_first(NC):
+            remote(ny.at[ci], ny.at[ci], s_n.at[0], r_n.at[0], on_y(i))
     with jax.named_scope("gram_z"):
         taken(gz.at[pl.ds(0, NZ - 1)], r_g.at[1])
         gy[ci] = sum(gz[z] for z in range(NZ))
         for i in far_first(NC):
             remote(gy.at[ci], gy.at[ci], s_g.at[2], r_g.at[2], on_y(i))
+    with jax.named_scope("cols1"):
+        rows_leave(1)
+        cols_first(1)
     with jax.named_scope("cols_second1"):
         cols_second(1)
-
-    with jax.named_scope("row_sum1"):
-        part = row_sum(1)
-    with jax.named_scope("cross"):
-        half = part - 0.5 * tr[:CH]
-        cross = sum(hdot(half[s * W : (s + 1) * W], allg[1, s], (1, 1)) for s in range(SEG))
-        ny[ci] = jnp.concatenate([cross[: W // 2], cross[W // 2 :]], 1)
-        for i in far_first(NC):
-            remote(ny.at[ci], ny.at[ci], s_n.at[0], r_n.at[0], on_y(i))
+    with jax.named_scope("cross_y"):
+        taken(ny.at[pl.ds(0, NC - 1)], r_n.at[0])
+        nz[zi] = sum(ny[c] for c in range(NC))
+        for i in far_first(NZ):
+            remote(nz.at[zi], nz.at[zi], s_n.at[1], r_n.at[1], on_z(i))
     with jax.named_scope("gram_y"):
         taken(gy.at[pl.ds(0, NC - 1)], r_g.at[2])
         piece = gx.at[ki * ND + di]
@@ -314,15 +358,16 @@
         for where in beside:
             remote(piece, piece, s_g.at[3], r_g.at[3], where)
     with jax.named_scope("col_sum1"):
-        part = part + col_sum(1)
+        part = row_sum(1) + col_sum(1)
         for s in range(SEG):
             allg[2, s, mine, :] = part[s * W : (s + 1) * W]
         x_gather(2)
-    with jax.named_scope("cross_y"):
-        taken(ny.at[pl.ds(0, NC - 1)], r_n.at[0])
-        nz[zi] = sum(ny[c] for c in range(NC))
-        for i in far_first(NZ):
-            remote(nz.at[zi], nz.at[zi], s_n.at[1], r_n.at[1], on_z(i))
+    with jax.named_scope("cross_z"):
+        taken(nz.at[pl.ds(0, NZ - 1)], r_n.at[1])
+        piece = nx.at[ki * ND + di]
+        nx[ki * ND + di] = sum(nz[z] for z in range(NZ))
+        for where in beside:
+            remote(piece, piece, s_n.at[2], r_n.at[2], where)
     with jax.named_scope("gram_x"):
         taken(gx.at[pl.ds(0, 2 * ND - 1)], r_g.at[3])
     with jax.named_scope("solve1"):
@@ -348,12 +393,6 @@
         known = hdot(lift, hdot(m1, lift, (1, 0)), (0, 0)) - mixed - mixed.T
         renewed_own = hdot(renewed, own, (1, 1))
         step_own = hdot(own, step, (1, 1))
-    with jax.named_scope("cross_z"):
-        taken(nz.at[pl.ds(0, NZ - 1)], r_n.at[1])
-        piece = nx.at[ki * ND + di]
-        nx[ki * ND + di] = sum(nz[z] for z in range(NZ))
-        for where in beside:
-            remote(piece, piece, s_n.at[2], r_n.at[2], where)
     with jax.named_scope("direction2"):
         for s in range(SEG):
             d2[s] = hdot(lift, allg[0, s], (0, 0)) - hdot(step, allg[1, s], (0, 0))
@@ -391,6 +430,7 @@
             taken(zb.at[it, pl.ds(0, NZ - 1)], s_z.at[it])
         for it in range(3):
             taken(allg.at[it, :, pl.ds(0, W * (ND - 1)), :], s_all.at[it])
+        taken(rowall.at[pl.ds(0, NC - 1), :, pl.ds(0, W * (ND - 1)), :], s_wide)
         taken(gb, s_g.at[0])
         taken(gz.at[pl.ds(0, NZ - 1)], s_g.at[1])
         taken(gy.at[pl.ds(0, NC - 1)], s_g.at[2])
@@ -407,7 +447,7 @@
     vm = lambda *shape: pltpu.VMEM(shape, F32)
     half = lambda *shape: pltpu.VMEM(shape, BF16)
     dma = lambda *shape: pltpu.SemaphoreType.DMA(shape)
-    shape = jax.ShapeDtypeStruct(right_sides.shape, F32)
+    shape = pltpu.VMEM(right_sides.shape, F32)
     return pl.pallas_call(
         functools.partial(kernel, dims),
         out_shape=(shape, shape),
@@ -416,14 +456,14 @@
         scratch_shapes=[
             vm(*right_sides.shape),
             vm(SLOTS, BLK, BLK), *[half(SLOTS, BLK, BLK)] * 4, half(NC * CH, SLOTS * W), half(2, NZ * CH, SLOTS * W),
-            *[vm(NC, SEG, W, BLK)] * 2, *[vm(2, NZ, SEG, W, BLK)] * 2, vm(3, SEG, NF, BLK),
+            *[vm(NC, SEG, W, BLK)] * 2, *[vm(2, NZ, SEG, W, BLK)] * 2, vm(3, SEG, NF, BLK), vm(NC, SEG, NF, BLK),
             vm(SLOTS * W, BLK), vm(SLOTS * W, BLK),
             vm(2, NC, CH, BLK), vm(2, 2, NZ, CH, BLK), vm(2, NC, CH, BLK), vm(2, NZ, CH, BLK), vm(2, NZ, CH, BLK),
             vm(2, W, 2 * NF), vm(W, 2 * NF), vm(NZ, W, 2 * NF), vm(NC, W, 2 * NF), vm(2 * ND, W, 2 * NF),
             vm(NC, W // 2, 2 * NF), vm(NZ, W // 2, 2 * NF), vm(2 * ND, W // 2, 2 * NF),
             vm(SEG, NF, BLK), vm(SEG, NF, BLK),
             dma(2),
-            dma(2), dma(2), dma(2), dma(3), dma(2), dma(2, NZ), dma(2), dma(3),
+            dma(2), dma(2), dma(2), dma(3), pltpu.SemaphoreType.DMA, dma(2, NC), dma(2, NZ), dma(2), dma(3), pltpu.SemaphoreType.DMA,
             dma(2), dma(2), dma(2), dma(2), dma(2), dma(2), dma(4), dma(4), dma(3), dma(3),
         ],
         compiler_params=pltpu.CompilerParams(

time: 75.7 us -> 77.9 us (1.029)
  Pallas kernels: 71.4 us -> 75.2 us
  local copies, waits for them, and re-layouts: 2.75 us -> 1.23 us
    pallas_call x1, Pallas kernels: 71.4 us -> 75.2 us  [per_device(): pl.pallas_call(functools.partial(kernel, dims), out_shape=(shape, shape),...]
    unnamed x2, local copies, waits for them, and re-layouts: 2.75 us -> 1.23 us
where the time goes in v3:
time: 77.9 us; the launch traced here: 77.7 us
  Pallas kernels  75.2 us (97%)
  between operations  1.29 us (2%)
  local copies, waits for them, and re-layouts  1.23 us (2%)
    pallas_call x1, Pallas kernels, per_device(): pl.pallas_call(functools.partial(kernel, dims), out_shape=(shape, shape),...  75.2 us

profile of v3, /device:TPU:1, one launch (start us, length us, event | category | flops | bytes accessed | tf_op | source)
XLA Modules:
  0.0 77.7 jit_solution(17067588609551883466)
XLA Ops:
  1.3 75.2 %block_cg.1 = (f32[16,512]{1,0:T(8,128)S(1)}, f32[16,512]{1,0:T(8,128)S(1)}) custom-call(f32[16,512]{1,0:T(8,128)} %rs_hbm.1, f32[16,256,256]{2,1,0:T(8,128)} %bitcast.1, s32[1,1,16]{2,1,0:T(1,128)} %rows_s.1, s32[1,1,16]{2,1,0:T(1,128)} %cols_s.1, s32[1,1]{1,0:T(1,128)S(6)} %copy.11.count_s), custom_call_target="tpu_custom_call" | custom-call | tf_op jit(solution)/shard_map/block_cg/pallas_call | solution.py:451
  76.5 0.6 copy.9
  77.1 0.6 copy.10

commit v4 on v2

--- a/solution.py
+++ b/solution.py
@@ -363,24 +363,6 @@
         taken(allg.at[2, :, pl.ds(0, W * (ND - 1)), :], r_all.at[2])
         for s in range(SEG):
             ad2[s] = hdot(lift, allg[1, s], (0, 0)) - hdot(step, allg[2, s], (0, 0))
-    with jax.named_scope("cross_x"):
-        taken(nx.at[pl.ds(0, 2 * ND - 1)], r_n.at[2])
-    with jax.named_scope("solve2"):
-        rows = []
-        for d in range(ND):
-            total = nx[d] + nx[ND + d]
-            rows += [total[:, :NF], total[:, NF:]]
-        cross = jnp.concatenate(rows, 0)
-        curvature = known + hdot(step, hdot(cross + cross.T, step, (1, 0)), (0, 0))
-        pad = jnp.zeros((NF, NF - W), F32)
-        (done,) = eliminate([jnp.concatenate([curvature, renewed_own, pad], 1)], NF)
-        step_own = done[:, NF : NF + W]
-    with jax.named_scope("finish"):
-        for s in range(SEG):
-            span = slice(s * BLK, (s + 1) * BLK)
-            x_ref[:, span] = x_ref[:, span] + hdot(step_own, d2[s], (0, 0))
-            r_ref[:, span] = r_ref[:, span] - hdot(step_own, ad2[s], (0, 0))
-
     with jax.named_scope("sent"):
         for it in range(2):
             taken(rowg[it].at[pl.ds(0, NC - 1)], s_row.at[it])
@@ -397,7 +379,25 @@
         taken(gx.at[pl.ds(0, 2 * ND - 1)], s_g.at[3])
         taken(ny.at[pl.ds(0, NC - 1)], s_n.at[0])
         taken(nz.at[pl.ds(0, NZ - 1)], s_n.at[1])
-        taken(nx.at[pl.ds(0, 2 * ND - 1)], s_n.at[2])
+    with jax.named_scope("cross_x"):
+        taken(nx.at[pl.ds(0, 2 * ND - 1)], r_n.at[2])
+    with jax.named_scope("solve2"):
+        rows = []
+        for d in range(ND):
+            total = nx[d] + nx[ND + d]
+            rows += [total[:, :NF], total[:, NF:]]
+        cross = jnp.concatenate(rows, 0)
+        curvature = known + hdot(step, hdot(cross + cross.T, step, (1, 0)), (0, 0))
+        pad = jnp.zeros((NF, NF - W), F32)
+        (done,) = eliminate([jnp.concatenate([curvature, renewed_own, pad], 1)], NF)
+        step_own = done[:, NF : NF + W]
+    with jax.named_scope("finish"):
+        for s in range(SEG):
+            span = slice(s * BLK, (s + 1) * BLK)
+            x_ref[:, span] = x_ref[:, span] + hdot(step_own, d2[s], (0, 0))
+            r_ref[:, span] = r_ref[:, span] - hdot(step_own, ad2[s], (0, 0))
+
+    taken(nx.at[pl.ds(0, 2 * ND - 1)], s_n.at[2])
 
 
 def per_device(dims, right_sides, blocks, block_rows, block_cols, block_count):
@@ -407,7 +407,7 @@
     vm = lambda *shape: pltpu.VMEM(shape, F32)
     half = lambda *shape: pltpu.VMEM(shape, BF16)
     dma = lambda *shape: pltpu.SemaphoreType.DMA(shape)
-    shape = jax.ShapeDtypeStruct(right_sides.shape, F32)
+    shape = pltpu.VMEM(right_sides.shape, F32)
     return pl.pallas_call(
         functools.partial(kernel, dims),
         out_shape=(shape, shape),

time: 75.7 us -> 73.4 us (0.970)
  local copies, waits for them, and re-layouts: 2.75 us -> 1.23 us
    unnamed x2, local copies, waits for them, and re-layouts: 2.75 us -> 1.23 us
where the time goes in v4:
time: 73.4 us; the launch traced here: 73.3 us
  Pallas kernels  70.8 us (96%)
  between operations  1.29 us (2%)
  local copies, waits for them, and re-layouts  1.23 us (2%)
    pallas_call x1, Pallas kernels, per_device(): pl.pallas_call(functools.partial(kernel, dims), out_shape=(shape, shape),...  70.8 us

profile of v4, /device:TPU:1, one launch (start us, length us, event | category | flops | bytes accessed | tf_op | source)
XLA Modules:
  0.0 73.3 jit_solution(15515967603901181136)
XLA Ops:
  1.3 70.8 %block_cg.1 = (f32[16,512]{1,0:T(8,128)S(1)}, f32[16,512]{1,0:T(8,128)S(1)}) custom-call(f32[16,512]{1,0:T(8,128)} %rs_hbm.1, f32[16,256,256]{2,1,0:T(8,128)} %bitcast.1, s32[1,1,16]{2,1,0:T(1,128)} %rows_s.1, s32[1,1,16]{2,1,0:T(1,128)} %cols_s.1, s32[1,1]{1,0:T(1,128)S(6)} %copy.11.count_s), custom_call_target="tpu_custom_call" | custom-call | tf_op jit(solution)/shard_map/block_cg/pallas_call | solution.py:411
  72.1 0.6 copy.9
  72.7 0.6 copy.10

commit v5 on v4

--- a/solution.py
+++ b/solution.py
@@ -36,14 +36,13 @@
 
 def eliminate(systems, n):
     m = systems[0].shape[1]
-    down = lax.broadcasted_iota(jnp.int32, (n, m), 0)
+    sub = lax.broadcasted_iota(jnp.int32, (PIVOTS, m), 0)
     spread = range(PIVOTS)
     for k in range(0, n, PIVOTS):
         after = []
         for a in systems:
-            rows = [jnp.broadcast_to(a[k + i : k + i + 1, :], (8, m)) for i in spread]
-            p = [[jnp.broadcast_to(rows[i][:, k + j : k + j + 1], (8, m)) for j in spread] for i in spread]
-            cols = [jnp.broadcast_to(a[:, k + j : k + j + 1], (n, m)) for j in spread]
+            rows = [jnp.broadcast_to(a[k + i : k + i + 1, :], (PIVOTS, m)) for i in spread]
+            p = [[jnp.broadcast_to(rows[i][:, k + j : k + j + 1], (PIVOTS, m)) for j in spread] for i in spread]
             for q in spread:
                 inverse = 1.0 / p[q][q]
                 rows[q] = rows[q] * inverse
@@ -54,13 +53,18 @@
                         for j in range(q + 1, PIVOTS):
                             p[i][j] = p[i][j] - p[i][q] * p[q][j]
                         rows[i] = rows[i] - p[i][q] * rows[q]
-            full = [jnp.concatenate([r] * (n // 8), 0) for r in rows]
-            new = a
-            for j in spread:
-                new = new - cols[j] * full[j]
-            for j in spread:
-                new = jnp.where(down == k + j, full[j], new)
-            after.append(new)
+            parts = []
+            for g in range(0, n, PIVOTS):
+                if g == k:
+                    part = rows[0]
+                    for j in range(1, PIVOTS):
+                        part = jnp.where(sub == j, rows[j], part)
+                else:
+                    part = a[g : g + PIVOTS]
+                    for j in spread:
+                        part = part - jnp.broadcast_to(a[g : g + PIVOTS, k + j : k + j + 1], (PIVOTS, m)) * rows[j]
+                parts.append(part)
+            after.append(jnp.concatenate(parts, 0))
         systems = after
     return systems
 
@@ -242,7 +246,7 @@
 
         lax.fori_loop(0, SLOTS, cut, 0)
     with jax.named_scope("forward0"):
-        forward(0, range(1, NZ))
+        forward(0, far_first(NZ))
     with jax.named_scope("wait_y0"):
         taken(rowg[0].at[pl.ds(0, NC - 1)], r_row.at[0])
     with jax.named_scope("cols0"):
@@ -274,7 +278,7 @@
         ga[0] = gram[:W]
         ga[1] = gram[W:]
         remote(ga.at[1 - ki], gb, s_g.at[0], r_g.at[0], sib)
-    order = sorted(range(1, NZ), key=lambda i: min(i, NZ - i))
+    order = far_first(NZ)
     with jax.named_scope("forward1"):
         forward(1, order[: len(order) // 2])
         taken(gb, r_g.at[0])

time: 73.4 us -> 72.8 us (level)
  no operation moved by 1% of the time
where the time goes in v5:
time: 72.8 us; the launch traced here: 72.6 us
  Pallas kernels  70.1 us (96%)
  between operations  1.29 us (2%)
  local copies, waits for them, and re-layouts  1.23 us (2%)
    pallas_call x1, Pallas kernels, per_device(): pl.pallas_call(functools.partial(kernel, dims), out_shape=(shape, shape),...  70.1 us

profile of v5, /device:TPU:1, one launch (start us, length us, event | category | flops | bytes accessed | tf_op | source)
XLA Modules:
  0.0 72.6 jit_solution(11887374871592029529)
XLA Ops:
  1.3 70.1 %block_cg.1 = (f32[16,512]{1,0:T(8,128)S(1)}, f32[16,512]{1,0:T(8,128)S(1)}) custom-call(f32[16,512]{1,0:T(8,128)} %rs_hbm.1, f32[16,256,256]{2,1,0:T(8,128)} %bitcast.1, s32[1,1,16]{2,1,0:T(1,128)} %rows_s.1, s32[1,1,16]{2,1,0:T(1,128)} %cols_s.1, s32[1,1]{1,0:T(1,128)S(6)} %copy.11.count_s), custom_call_target="tpu_custom_call" | custom-call | tf_op jit(solution)/shard_map/block_cg/pallas_call | solution.py:415
  71.4 0.6 copy.9
  72.0 0.6 copy.10

commit v6 on v5

--- a/solution.py
+++ b/solution.py
@@ -280,12 +280,11 @@
         remote(ga.at[1 - ki], gb, s_g.at[0], r_g.at[0], sib)
     order = far_first(NZ)
     with jax.named_scope("forward1"):
-        forward(1, order[: len(order) // 2])
+        forward(1, order)
         taken(gb, r_g.at[0])
         gz[zi] = ga[ki] + gb[...]
         for i in far_first(NZ):
             remote(gz.at[zi], gz.at[zi], s_g.at[1], r_g.at[1], on_z(i))
-        forward(1, order[len(order) // 2 :])
     with jax.named_scope("wait_sib1"):
         taken(colg[1].at[1 - ki], r_sib.at[1])
     with jax.named_scope("rows1"):

time: 72.8 us -> 72.7 us (level)
  no operation moved by 1% of the time
where the time goes in v6:
time: 72.7 us; the launch traced here: 72.6 us
  Pallas kernels  70 us (96%)
  between operations  1.29 us (2%)
  local copies, waits for them, and re-layouts  1.23 us (2%)
    pallas_call x1, Pallas kernels, per_device(): pl.pallas_call(functools.partial(kernel, dims), out_shape=(shape, shape),...  70 us

profile of v6, /device:TPU:1, one launch (start us, length us, event | category | flops | bytes accessed | tf_op | source)
XLA Modules:
  0.0 72.6 jit_solution(6825884575437774164)
XLA Ops:
  1.3 70.0 %block_cg.1 = (f32[16,512]{1,0:T(8,128)S(1)}, f32[16,512]{1,0:T(8,128)S(1)}) custom-call(f32[16,512]{1,0:T(8,128)} %rs_hbm.1, f32[16,256,256]{2,1,0:T(8,128)} %bitcast.1, s32[1,1,16]{2,1,0:T(1,128)} %rows_s.1, s32[1,1,16]{2,1,0:T(1,128)} %cols_s.1, s32[1,1]{1,0:T(1,128)S(6)} %copy.11.count_s), custom_call_target="tpu_custom_call" | custom-call | tf_op jit(solution)/shard_map/block_cg/pallas_call | solution.py:414
  71.3 0.6 copy.9
  71.9 0.6 copy.10
